TPU v7x, 128 devices: a whole 4x4x4 slice. The times are simulated.
128 devices in a mesh: grp: 8 (over y, core), mid: 16 (over x, z).
Axes of the slice: x: 4, y: 4, z: 4, core: 2. Of those that a mesh axis runs over, the one named last changes fastest.
Arguments:
- queries: bfloat16 [16384, 768], P('grp'), may hold values from -6 to 6
- coarse_vectors: bfloat16 [2048, 768], replicated, may hold values from -0.4375 to 0.4375
- mid_vectors: bfloat16 [262144, 768], P(('grp', 'mid')), may hold values from -0.4375 to 0.4375
- leaf_vectors: bfloat16 [131072, 768], P(('grp', 'mid')), may hold values from -0.4375 to 0.4375
- coarse_pos: int32 [16384, 4], P(('grp', 'mid')), may hold values from 0 to 2047
- mid_pos: int32 [16384, 4], P('grp'), may hold values from 0 to 4095
- leaf_pos: int32 [16384, 4], P('grp'), may hold values from 0 to 4095
- mid_cand: int32 [128, 8], P('grp'), may hold values from 0 to 511, as said below
- leaf_cand: int32 [128, 8], P('grp'), may hold values from 0 to 255, as said below
- leaf_owner: int32 [256], replicated, may hold values from 0 to 255, as said below
Outputs:
- grad_query: float32 [16384, 768], P(('grp', 'mid'))
- grad_coarse: float32 [2048, 768], P(('grp', 'mid'))
- grad_mid: float32 [262144, 768], P(('grp', 'mid'))
- grad_leaf: float32 [131072, 768], P(('grp', 'mid'))
Inputs may be any that keep to these rules, and one draw needn't show every extreme that they name: `mid_cand`: mid block b lies on device b // 4 in grp+mid order. Among the candidates of the tiles of one group, at most 2 lie on devices of one mid index within one group; in every draw some device receives 2 such candidates from every group. `leaf_cand`: storage block s lies on device s // 2 in grp+mid order. Among the candidates of the tiles of one group, at most 2 are stored on devices of one mid index within one group; in every draw some device receives 2 such candidates from every group. `leaf_owner`: A permutation of the leaf blocks.
All inputs are finite; a program needn't handle non-finite values.
Results may differ from a plain program's by a relative error of at most 0.0065.
Values may be sent and summed in bfloat16 or wider, within the bound.
A program may use at most 256 MiB of HBM per device.

v0:
```python
import jax
import jax.numpy as jnp
from jax import lax
from jax.sharding import PartitionSpec as P

TILE = 128
BLOCK = 512
COARSE = 2048
K_CAND = 8
POS = 4


loss_scale = 0.25


def targets(relative, span):
    columns = jnp.arange(span, dtype=jnp.int32)
    return jnp.any(relative[..., None] == columns, axis=-2).astype(jnp.float32)


def shards(
    queries,
    coarse_vectors,
    mid_vectors,
    leaf_vectors,
    coarse_pos,
    mid_pos,
    leaf_pos,
    mid_cand,
    leaf_cand,
    leaf_owner,
):
    grp_count = lax.axis_size("grp")
    mid_count = lax.axis_size("mid")
    mid_index = lax.axis_index("mid")
    group_rows, feature = queries.shape
    dev_queries = group_rows // mid_count
    group_tiles = group_rows // TILE
    capacity = max(2, (2 * dev_queries * K_CAND // TILE + grp_count - 1) // grp_count)
    own_rows = lax.dynamic_slice_in_dim(queries, mid_index * dev_queries, dev_queries, 0)
    coarse_scores = lax.dot_general(
        own_rows, coarse_vectors, (((1,), (1,)), ((), ())), preferred_element_type=jnp.float32
    )
    coarse_delta = (
        (jax.nn.sigmoid(coarse_scores) - targets(coarse_pos, COARSE)) * loss_scale
    ).astype(jnp.bfloat16)
    query_coarse = jnp.dot(coarse_delta, coarse_vectors, preferred_element_type=jnp.float32)
    grad_coarse = lax.psum_scatter(
        lax.dot_general(
            coarse_delta, own_rows, (((0,), (0,)), ((), ())), preferred_element_type=jnp.float32
        ),
        ("grp", "mid"),
        scatter_dimension=0,
        tiled=True,
    )
    mid_blocks = mid_vectors.shape[0] // BLOCK
    leaf_blocks = leaf_vectors.shape[0] // BLOCK
    storage = jnp.concatenate(
        [
            mid_vectors.reshape(mid_blocks, BLOCK, feature),
            leaf_vectors.reshape(leaf_blocks, BLOCK, feature),
        ],
        axis=0,
    )
    block_total = mid_blocks + leaf_blocks
    table_size = leaf_owner.shape[0]
    leaf_match = leaf_cand[..., None] == jnp.arange(table_size, dtype=jnp.int32)
    leaf_storage = jnp.sum(jnp.where(leaf_match, leaf_owner, 0), axis=-1)
    tile_queries = queries.reshape(group_tiles, TILE, feature)

    def route_plan(candidates, positives, per_device, offset):
        flat_ids = candidates.reshape(-1)
        pair_count = flat_ids.shape[0]
        owner_dev = flat_ids // per_device
        target_grp = owner_dev // mid_count
        is_mine = owner_dev % mid_count == mid_index
        ordinal = jnp.arange(pair_count, dtype=jnp.int32)
        earlier = (
            (target_grp[:, None] == target_grp[None, :])
            & is_mine[None, :]
            & (ordinal[None, :] < ordinal[:, None])
        )
        slot_rank = jnp.sum(earlier.astype(jnp.int32), axis=1)
        picked = (
            is_mine[None, None, :]
            & (target_grp[None, None, :] == jnp.arange(grp_count, dtype=jnp.int32)[:, None, None])
            & (slot_rank[None, None, :] == jnp.arange(capacity, dtype=jnp.int32)[None, :, None])
        )
        is_valid = jnp.any(picked, axis=2)
        pair_index = jnp.sum(jnp.where(picked, ordinal, 0), axis=2)
        tile_index = pair_index // K_CAND
        cand_index = pair_index % K_CAND
        tile_rows = tile_queries[tile_index]
        relative = (
            positives.reshape(group_tiles, TILE, POS)[tile_index]
            - (cand_index * BLOCK)[:, :, None, None]
        )
        block_slot = jnp.where(is_valid, flat_ids[pair_index] % per_device + offset, -1)
        return (tile_rows, relative, block_slot, tile_index, is_valid)

    mid_plan = route_plan(mid_cand, mid_pos, mid_blocks, 0)
    leaf_plan = route_plan(leaf_storage, leaf_pos, leaf_blocks, mid_blocks)
    tile_rows = jnp.concatenate([mid_plan[0], leaf_plan[0]], axis=1)
    relative = jnp.concatenate([mid_plan[1], leaf_plan[1]], axis=1)
    block_slot = jnp.concatenate([mid_plan[2], leaf_plan[2]], axis=1)
    tile_index = jnp.concatenate([mid_plan[3], leaf_plan[3]], axis=1)
    is_valid = jnp.concatenate([mid_plan[4], leaf_plan[4]], axis=1)
    request_rows = lax.all_to_all(tile_rows, "grp", split_axis=0, concat_axis=0, tiled=True)
    request_relative = lax.all_to_all(relative, "grp", split_axis=0, concat_axis=0, tiled=True)
    request_slot = lax.all_to_all(block_slot, "grp", split_axis=0, concat_axis=0, tiled=True)
    vectors = storage[jnp.maximum(request_slot, 0)]
    scores = jnp.einsum(
        "gnqd,gnld->gnql", request_rows, vectors, preferred_element_type=jnp.float32
    )
    is_live = (request_slot >= 0)[..., None, None]
    delta = jnp.where(
        is_live, (jax.nn.sigmoid(scores) - targets(request_relative, BLOCK)) * loss_scale, 0.0
    ).astype(jnp.bfloat16)
    query_terms = jnp.einsum(
        "gnql,gnld->gnqd", delta, vectors, preferred_element_type=jnp.float32
    ).astype(jnp.bfloat16)
    block_terms = jnp.einsum(
        "gnql,gnqd->gnld", delta, request_rows, preferred_element_type=jnp.float32
    )
    returned = lax.all_to_all(query_terms, "grp", split_axis=0, concat_axis=0, tiled=True)
    returned, block_terms, received_slot = (returned, block_terms, request_slot)
    block_onehot = (received_slot[..., None] == jnp.arange(block_total, dtype=jnp.int32)).astype(
        jnp.float32
    )
    block_grads = jnp.einsum(
        "gnb,gnld->bld", block_onehot, block_terms, precision=lax.Precision.HIGHEST
    )
    grad_mid = block_grads[:mid_blocks].reshape(mid_blocks * BLOCK, feature)
    grad_leaf = block_grads[mid_blocks:].reshape(leaf_blocks * BLOCK, feature)
    tile_onehot = (
        (tile_index[..., None] == jnp.arange(group_tiles, dtype=jnp.int32)) & is_valid[..., None]
    ).astype(jnp.bfloat16)
    partial_value = jnp.einsum(
        "gnt,gnqd->tqd", tile_onehot, returned, preferred_element_type=jnp.float32
    ).reshape(group_rows, feature)
    grad_query = (
        lax.psum_scatter(partial_value, "mid", scatter_dimension=0, tiled=True) + query_coarse
    )
    return (grad_query, grad_coarse, grad_mid, grad_leaf)


def solution(mesh):
    placed = (
        P("grp", None),
        P(),
        P(("grp", "mid"), None),
        P(("grp", "mid"), None),
        P(("grp", "mid"), None),
        P("grp", None),
        P("grp", None),
        P("grp", None),
        P("grp", None),
        P(),
    )
    return jax.shard_map(
        shards,
        mesh=mesh,
        in_specs=placed,
        out_specs=(
            P(("grp", "mid"), None),
            P(("grp", "mid"), None),
            P(("grp", "mid"), None),
            P(("grp", "mid"), None),
        ),
        check_vma=False,
    )
```

profile of v0, /device:TPU:0, one launch (start us, length us, event | category | flops | bytes accessed | tf_op | source)
XLA Modules:
  0.0 558.5 jit_solution(6255425457671670305)
XLA Ops:
  14.0 4.6 all-to-all-start
  25.9 4.8 all-to-all-start.2
  30.7 6.1 %pad_maximum_fusion = bf16[8,4,128,768]{3,2,1,0:T(8,128)(2,1)} fusion(bf16[8,2,128,768]{3,2,1,0:T(8,128)(2,1)} %bitcast.77, bf16[8,2,128,768]{3,2,1,0:T(8,128)(2,1)} %bitcast.76), kind=kLoop, calls=%fused_computation.14 | loop fusion | flops 3145728 | bytes 12582912 | tf_op jit(solution)/shard_map/concatenate | solution.py:103
  36.8 5.4 all-to-all-start.1
  42.2 4.9 pad_maximum_fusion.1
  47.4 12.4 %gather_fusion.4 = bf16[32,512,768]{2,1,0:T(8,128)(2,1)} fusion(bf16[6,512,768]{2,1,0:T(8,128)(2,1)} %pad_maximum_fusion.1, s32[1024]{0:T(1024)S(1)} %pad_clamp_fusion), kind=kCustom, calls=%fused_computation.4 | custom fusion | bytes 50331776 | tf_op jit(solution)/shard_map/gather | solution.py:111
  59.8 7.3 %fusion.2 = pred[8,4,128,512]{3,2,1,0:T(8,128)(4,1)} fusion(s32[8,4,128,4]{2,3,1,0:T(4,128)S(1)} %all-to-all-done.2), kind=kLoop, calls=%fused_computation.10 | loop fusion | flops 14680064 | bytes 2162688 | tf_op jit(solution)/shard_map/reduce_or | solution.py:18
  67.1 47.3 %all-to-all-done.1 = bf16[8,4,128,768]{3,2,1,0:T(8,128)(2,1)} async-done(((bf16[8,4,128,768]{3,2,1,0:T(8,128)(2,1)}), bf16[8,4,128,768]{3,2,1,0:T(8,128)(2,1)}, u32[]{:S(2)}, u32[]{:S(2)}) %all-to-all-start.1) | async-done | bytes 6291488 | tf_op jit(solution)/shard_map/all_to_all | solution.py:108
  114.4 16.8 %fusion.63 = f32[8,4,128,512]{3,2,1,0:T(8,128)} fusion(bf16[8,4,128,768]{3,2,1,0:T(8,128)(2,1)} %all-to-all-done.1, bf16[8,4,512,768]{3,2,1,0:T(8,128)(2,1)} %bitcast.69), kind=kOutput, calls=%fused_computation.151 | convolution fusion | flops 3221225472 | bytes 39845888 | tf_op jit(solution)/shard_map/gnqd,gnld->gnql/dot_general | solution.py:112
  131.2 20.2 %fusion.19 = bf16[8,4,128,768]{3,2,1,0:T(8,128)(2,1)} fusion(bf16[8,4,512,768]{3,2,1,0:T(8,128)(2,1)} %bitcast.70, pred[8,4,128,512]{3,2,1,0:T(8,128)(4,1)} %fusion.2, f32[8,4,128,512]{3,2,1,0:T(8,128)} %fusion.63, pred[8,4]{1,0:T(8,128)(4,1)S(1)} %copy.82), kind=kOutput, calls=%fused_computation.29 | convolution fusion | flops 3241148416 | bytes 41943072 | tf_op jit(solution)/shard_map/gnql,gnld->gnqd/dot_general | solution.py:119
  151.4 10.3 %copy.87 = bf16[8,4,128,768]{3,1,2,0:T(4,128)(2,1)} copy(bf16[8,4,128,768]{3,2,1,0:T(8,128)(2,1)} %fusion.19) | data formatting | bytes 12582912 | tf_op jit(solution)/shard_map/convert_element_type | solution.py:121
  161.7 4.7 all-to-all-start.3
  166.6 72.1 %all-to-all-done.3 = bf16[8,4,128,768]{3,1,2,0:T(4,128)(2,1)} async-done(((bf16[8,4,128,768]{3,1,2,0:T(4,128)(2,1)}), bf16[8,4,128,768]{3,1,2,0:T(4,128)(2,1)}, u32[]{:S(2)}, u32[]{:S(2)}) %all-to-all-start.3) | async-done | bytes 6291488 | tf_op jit(solution)/shard_map/all_to_all | solution.py:125
  238.6 7.1 %fusion.20 = f32[16,128,768]{2,0,1:T(8,128)S(1)} fusion(bf16[8,4,128,768]{3,1,2,0:T(4,128)(2,1)} %all-to-all-done.3, s32[8,4]{0,1:T(4,128)S(1)} %pad_add_fusion.1, pred[8,4]{0,1:T(4,128)(4,1)S(1)} %pad_add_fusion.2), kind=kOutput, calls=%fused_computation.30 | convolution fusion | flops 100664320 | bytes 12583072 | tf_op jit(solution)/shard_map/gnt,gnqd->tqd/dot_general | solution.py:138
  245.7 6.2 %copy.89 = f32[16,128,768]{2,1,0:T(8,128)} copy(f32[16,128,768]{2,0,1:T(8,128)S(1)} %fusion.20) | data formatting | bytes 12582912 | tf_op jit(solution)/shard_map/gnt,gnqd->tqd/dot_general | solution.py:138
  253.6 3.1 fusion.28
  257.5 3.7 fusion.29
  261.2 24.8 %fusion.3 = f32[8,4,512,768]{3,2,1,0:T(8,128)} fusion(bf16[8,4,128,768]{3,2,1,0:T(8,128)(2,1)} %all-to-all-done.1, pred[8,4,128,512]{3,2,1,0:T(8,128)(4,1)} %fusion.2, f32[8,4,128,512]{3,2,1,0:T(8,128)} %fusion.63, pred[8,4]{1,0:T(8,128)(4,1)S(1)} %copy.82), kind=kOutput, calls=%fused_computation.12 | convolution fusion | flops 3238002688 | bytes 67108896 | tf_op jit(solution)/shard_map/gnql,gnqd->gnld/dot_general | solution.py:122
  286.0 64.0 %fusion.7 = f32[6,512,768]{2,0,1:T(8,128)} fusion(f32[8,4,512,768]{3,2,1,0:T(8,128)} %fusion.3, s32[8,4]{0,1:T(4,128)S(1)} %bitcast.82), kind=kOutput, calls=%fused_computation.18 | convolution fusion | flops 905969856 | bytes 59768960 | tf_op jit(solution)/shard_map/gnb,gnld->bld/dot_general | solution.py:130
  350.0 6.3 %slice.23 = f32[2,512,768]{2,0,1:T(2,128)S(1)} slice(f32[6,512,768]{2,0,1:T(8,128)} %fusion.7), slice={[4:6], [0:512], [0:768]} | slice | bytes 6291456 | tf_op jit(solution)/shard_map/slice | solution.py:134
  356.4 8.4 %slice.22 = f32[4,512,768]{2,0,1:T(4,128)} slice(f32[6,512,768]{2,0,1:T(8,128)} %fusion.7), slice={[0:4], [0:512], [0:768]} | slice | bytes 12582912 | tf_op jit(solution)/shard_map/slice | solution.py:133
  364.8 6.8 %copy.92 = f32[4,512,768]{2,1,0:T(8,128)} copy(f32[4,512,768]{2,0,1:T(4,128)} %slice.22) | data formatting | bytes 12582912 | tf_op jit(solution)/shard_map/slice | solution.py:133
  373.5 3.5 convolution_add_fusion
  377.0 174.4 %reduce-scatter.5.cloned.1.call-done = f32[16,768]{1,0:T(8,128)} async-done(((f32[2048,768]{1,0:T(8,128)}), f32[16,768]{1,0:T(8,128)}) %reduce-scatter.5.cloned.1.call-update) | async-done | bytes 49168 | tf_op jit(solution)/shard_map/reduce_scatter | solution.py:48
  (80 shorter events, 18.7 us)
Async XLA Ops:
  7.2 13.9 %copy-start = (bf16[2048,768]{1,0:T(8,128)(2,1)S(1)}, bf16[2048,768]{1,0:T(8,128)(2,1)}, u32[]{:S(2)}) copy-start(bf16[2048,768]{1,0:T(8,128)(2,1)} %param.10) | copy-start | bytes 9437188
  7.2 11.9 %copy-start.1 = (s32[2048,4]{0,1:T(4,128)S(1)}, s32[2048,4]{0,1:T(4,128)}, u32[]{:S(2)}) copy-start(s32[2048,4]{0,1:T(4,128)} %param.16) | copy-start | bytes 98308
  7.2 12.6 %copy-start.2 = (s32[2048,4]{0,1:T(4,128)S(1)}, s32[2048,4]{0,1:T(4,128)}, u32[]{:S(2)}) copy-start(s32[2048,4]{0,1:T(4,128)} %param.15) | copy-start | bytes 98308
  14.0 11.9 %all-to-all-start = ((s32[8,1,4]{2,1,0:T(1,128)}), s32[8,1,4]{2,1,0:T(1,128)S(1)}, u32[]{:S(2)}, u32[]{:S(2)}) async-start(s32[8,1,4]{2,1,0:T(1,128)} %copy.80), calls=%async_computation | async-start | bytes 8192 | tf_op jit(solution)/shard_map/all_to_all | solution.py:110
  25.9 10.9 %all-to-all-start.2 = ((s32[8,4,128,4]{2,3,1,0:T(4,128)}), s32[8,4,128,4]{2,3,1,0:T(4,128)S(1)}, u32[]{:S(2)}, u32[]{:S(2)}) async-start(s32[8,4,128,4]{2,3,1,0:T(4,128)} %pad_add_fusion), calls=%async_computation.2 | async-start | bytes 131072 | tf_op jit(solution)/shard_map/all_to_all | solution.py:109
  36.8 77.6 %all-to-all-start.1 = ((bf16[8,4,128,768]{3,2,1,0:T(8,128)(2,1)}), bf16[8,4,128,768]{3,2,1,0:T(8,128)(2,1)}, u32[]{:S(2)}, u32[]{:S(2)}) async-start(bf16[8,4,128,768]{3,2,1,0:T(8,128)(2,1)} %pad_maximum_fusion), calls=%async_computation.1 | async-start | bytes 12582912 | tf_op jit(solution)/shard_map/all_to_all | solution.py:108
  161.7 76.9 %all-to-all-start.3 = ((bf16[8,4,128,768]{3,1,2,0:T(4,128)(2,1)}), bf16[8,4,128,768]{3,1,2,0:T(4,128)(2,1)}, u32[]{:S(2)}, u32[]{:S(2)}) async-start(bf16[8,4,128,768]{3,1,2,0:T(4,128)(2,1)} %copy.87), calls=%async_computation.3 | async-start | bytes 12582912 | tf_op jit(solution)/shard_map/all_to_all | solution.py:125
  166.5 207.0 %reduce-scatter.3.cloned.1.call-start = ((), (), s32[]{:S(2)}) async-start(), calls=%async_computation.6 | async-start | bytes 6684672 | tf_op jit(solution)/shard_map/reduce_scatter | solution.py:142
  251.9 0.7 copy-start.4
  252.0 299.4 %reduce-scatter.5.cloned.1.call-start = ((), (), s32[]{:S(2)}) async-start(), calls=%async_computation.7 | async-start | bytes 6340608 | tf_op jit(solution)/shard_map/reduce_scatter | solution.py:48
  256.7 0.8 copy-start.3
Sparse Core Ops, SparseCore 0:
  252.1 81.8 reduce-scatter.2
  339.5 211.8 reduce-scatter.4
where the time goes:
time: 562 us; the launch traced here: 559 us
  waiting for transfers between devices  294 us (52%)
  matrix products  143 us (25%)
  local copies, waits for them, and re-layouts  64.8 us (12%)
  other arithmetic  22.4 us (4%)
  starting transfers between devices  19.8 us (4%)
  between operations  14.6 us (3%)
    reduce_scatter x1, waiting for transfers between devices, shards(): lax.psum_scatter(lax.dot_general(coarse_delta, own_rows, (((0,), (0,)), (...  174 us
    all_to_all x1, waiting for transfers between devices, shards(): lax.all_to_all(query_terms, 'grp', split_axis=0, concat_axis=0, tiled=True)  72.1 us
    dot_general x1, matrix products, shards(): jnp.einsum('gnb,gnld->bld', block_onehot, block_terms, precision=lax.Prec...  64 us
    all_to_all x1, waiting for transfers between devices, shards(): lax.all_to_all(tile_rows, 'grp', split_axis=0, concat_axis=0, tiled=True)  47.3 us
    dot_general x1, matrix products, shards(): jnp.einsum('gnql,gnqd->gnld', delta, request_rows, preferred_element_type...  24.8 us
    dot_general x1, matrix products, shards(): jnp.einsum('gnql,gnld->gnqd', delta, vectors, preferred_element_type=jnp....  20.2 us
    dot_general x1, matrix products, shards(): jnp.einsum('gnqd,gnld->gnql', request_rows, vectors, preferred_element_ty...  16.8 us
    slice x2, local copies, waits for them, and re-layouts, shards(): grad_mid = block_grads[:mid_blocks].reshape(mid_blocks * BLOCK, feature)  15.2 us
  transfers between devices with their start and end apart: 6, of which 3 were waited for; matrix products, arithmetic and copies ran while one was open for 29% of the time, Pallas kernels for 0%

commit v1 on v0

v1 whole, which is shorter than its diff:
```python
import jax
import jax.numpy as jnp
from jax import lax
from jax.experimental import pallas as pl
from jax.experimental.pallas import tpu as pltpu
from jax.sharding import PartitionSpec as P

TILE = 128
BLOCK = 512
COARSE = 2048
K_CAND = 8
D = 768
NY, NX, NZ = 4, 4, 4
TILES = NX * NZ
BIG = 1 << 20
F32 = jnp.float32
BF16 = jnp.bfloat16
MESH = pl.DeviceIdType.MESH
R0, R1, R2 = (0, 32), (32, 48), (80, 48)
ROWS0, ROWS1, ROWS2 = pl.ds(*R0), pl.ds(*R1), pl.ds(*R2)
THIRD = D // 3
HALF = D // 2


def mm(a, b, ca, cb):
    return lax.dot_general(a, b, (((ca,), (cb,)), ((), ())), preferred_element_type=F32)


def delta_of(scores, labels, positives):
    hit = labels == positives[0:1]
    for p in range(1, 4):
        hit = hit | (labels == positives[p : p + 1])
    return (0.125 * jnp.tanh(0.5 * scores) + jnp.where(hit, -0.125, 0.125)).astype(BF16)


class Place:
    def __init__(self):
        grp, mid = lax.axis_index("grp"), lax.axis_index("mid")
        self.y, self.c = grp // 2, lax.rem(grp, 2)
        self.x, self.z = mid // NZ, lax.rem(mid, NZ)
        self.mid = mid
        self.ahead = 1 + 2 * self.c
        self.behind = 3 - 2 * self.c

    def at(self, dy=0, dx=0, dz=0):
        y, x, z = lax.rem(self.y + dy, NY), lax.rem(self.x + dx, NX), lax.rem(self.z + dz, NZ)
        return (2 * y + self.c, NZ * x + z)

    def sibling(self):
        return (2 * self.y + 1 - self.c, self.mid)

    def tile(self, dx, dz):
        return NZ * lax.rem(self.x + dx, NX) + lax.rem(self.z + dz, NZ)

    def greet(self):
        near = [self.sibling()]
        for step in (self.ahead, self.behind):
            near += [self.at(dy=step), self.at(dx=step), self.at(dz=step)]
        barrier = pltpu.get_barrier_semaphore()
        for device in near:
            pl.semaphore_signal(barrier, inc=1, device_id=device, device_id_type=MESH)
        pl.semaphore_wait(barrier, len(near))


class Net:
    def __init__(self, send_sem, recv_sem):
        self.send_sem, self.recv_sem, self.made = send_sem, recv_sem, []

    def send(self, src, dst, device):
        i = len(self.made)
        copy = pltpu.make_async_remote_copy(
            src_ref=src,
            dst_ref=dst,
            send_sem=self.send_sem.at[i],
            recv_sem=self.recv_sem.at[i],
            device_id=device,
            device_id_type=MESH,
        )
        copy.start()
        self.made.append(copy)
        return copy

    def finish(self):
        for copy in self.made:
            copy.wait_send()


COPIES = 200
OWN, BACK, FRONT, ACROSS = range(4)
SLOTS = 32


def role_step(color, role):
    return (0, 3 - 2 * color, 1 + 2 * color, 2)[role]


def main_kernel(
    q, mp, lp, mc, lc, cp, owner, cv, midv, leafv,
    gq, gco, sel, deltas, plan,
    q_own, q_b, q_a, q_2, p_own, p_b, p_a, p_2, cvv, cvm, cpall, packo, packs, packr,
    metao, metas, metar, planv, planr, plans, planrs, vectors, held_delta, gc, qc,
    own0, own1, own2, own3, sib0, sib1, sib2, sib3, gsib, gbuf,
    s2, sb, r2, rb, ra, u2, ub, ua, w2, wb, wa, local_sem, send_sem, recv_sem,
):
    me = Place()
    c, a, b = me.c, me.ahead, me.behind
    net = Net(send_sem, recv_sem)
    local = []

    def start_local(src, dst):
        copy = pltpu.make_async_copy(src, dst, local_sem.at[len(local)])
        copy.start()
        local.append(copy)
        return copy

    load_q = start_local(q, q_own)
    load_v = [start_local(midv, vectors.at[pl.ds(0, 4)]), start_local(leafv, vectors.at[pl.ds(4, 2)])]
    load_c = start_local(cv, cvv)
    for t in range(TILES):
        p_own[t, 0:4, :] = mp[:, t * TILE : (t + 1) * TILE]
        p_own[t, 4:8, :] = lp[:, t * TILE : (t + 1) * TILE]
    p_own[16:18] = jnp.full((2, 8, 128), -1, jnp.int32)
    p_own[16, :, 0:TILES] = mc[...]
    p_own[17, :, 0:TILES] = lc[...]
    cpall[me.x, me.z, 0:4, :] = cp[...]
    cpall[me.x, me.z, 4:8, :] = cp[...]
    me.greet()

    m = me.mid
    small = pl.ds(R1[0], R1[1] + R2[1])
    up, down = me.at(dy=a), me.at(dy=b)
    xa, xb, za, zb = me.at(dx=a), me.at(dx=b), me.at(dz=a), me.at(dz=b)
    sib = me.sibling()
    planes = {BACK: q_b, FRONT: q_a, ACROSS: q_2}

    y_a = net.send(q.at[m, small], q_b.at[m, small], up)
    y_b = net.send(q.at[m, small], q_a.at[m, small], down)
    at_y = {BACK: y_a, FRONT: y_b}
    pos_own = cpall.at[me.x, me.z]
    cz_a = net.send(pos_own, pos_own, za)
    cz_b = net.send(pos_own, pos_own, zb)
    pr_a = net.send(p_own, p_b, up)
    pr_b = net.send(p_own, p_a, down)

    def bulk(i):
        return pl.ds(4 * i, 4)

    t0_a, t0_b, t0_f = [], [], []

    def bulk_own(i):
        t0_a.append(net.send(q.at[bulk(i), ROWS0], q_b.at[bulk(i), ROWS0], up))
        t0_b.append(net.send(q.at[bulk(i), ROWS0], q_a.at[bulk(i), ROWS0], down))

    def bulk_forward(i):
        t0_a[i].wait_recv()
        t0_f.append(net.send(q_b.at[bulk(i), ROWS0], q_2.at[bulk(i), ROWS0], up))

    bulk_own(0)

    axes = ((ROWS1, za, zb, xa, xb), (ROWS2, xa, xb, za, zb))

    def tile_of(h, first, last):
        return me.tile(last, first) if h == 0 else me.tile(first, last)

    second, second_f, last, last_f = {}, {}, {}, {}
    walk = (0, b, a, 2)

    def send_second(role):
        for h, (rows, to_a, to_b, _, _) in enumerate(axes):
            piece = planes[role].at[m, rows]
            second[role, h] = (net.send(piece, piece, to_a), net.send(piece, piece, to_b))

    def send_last(role, key):
        step = walk[key]
        for h, (rows, _, _, to_a, to_b) in enumerate(axes):
            piece = planes[role].at[tile_of(h, step, 0), rows]
            last[role, h, key] = (net.send(piece, piece, to_a), net.send(piece, piece, to_b))

    def second_stage(role):
        for h, (rows, to_a, _, _, _) in enumerate(axes):
            second[role, h][0].wait_recv()
            piece = planes[role].at[tile_of(h, b, 0), rows]
            second_f[role, h] = net.send(piece, piece, to_a)
        send_last(role, BACK)
        for h in range(2):
            second[role, h][1].wait_recv()
        send_last(role, FRONT)

    def across_stage(role):
        for h in range(2):
            second_f[role, h].wait_recv()
        send_last(role, ACROSS)

    def forward_last(role):
        for key, step in enumerate(walk):
            for h, (rows, _, _, to_a, _) in enumerate(axes):
                last[role, h, key][0].wait_recv()
                piece = planes[role].at[tile_of(h, step, b), rows]
                last_f[role, h, key] = net.send(piece, piece, to_a)

    def complete(role):
        for key in range(4):
            for h in range(2):
                last[role, h, key][1].wait_recv()
                last_f[role, h, key].wait_recv()

    y_a.wait_recv()
    y_f = net.send(q_b.at[m, small], q_2.at[m, small], up)
    send_second(BACK)
    y_b.wait_recv()
    send_second(FRONT)
    cz_a.wait_recv()
    pos_b = cpall.at[me.x, lax.rem(me.z + b, NZ)]
    cz_f = net.send(pos_b, pos_b, za)
    pr_a.wait_recv()
    pr_f = net.send(p_b, p_2, up)
    bulk_own(1)
    send_last(BACK, OWN)
    second_stage(BACK)
    y_f.wait_recv()
    send_second(ACROSS)
    bulk_own(2)
    bulk_own(3)
    across_stage(BACK)
    send_last(FRONT, OWN)
    second_stage(FRONT)
    cz_b.wait_recv()
    cz_f.wait_recv()
    pos_row = cpall.at[me.x]
    cx_a = net.send(pos_row, pos_row, xa)
    cx_b = net.send(pos_row, pos_row, xb)
    bulk_forward(0)
    pr_b.wait_recv()
    pr_f.wait_recv()
    index = lax.broadcasted_iota(jnp.int32, (2, 128), 0) * 128 + lax.broadcasted_iota(
        jnp.int32, (2, 128), 1
    )
    code = 4 * (
        TILES * lax.broadcasted_iota(jnp.int32, (8, 128), 0)
        + lax.broadcasted_iota(jnp.int32, (8, 128), 1)
    )
    lane = lax.broadcasted_iota(jnp.int32, (1, 128), 1)
    tables = {OWN: p_own, BACK: p_b, FRONT: p_a, ACROSS: p_2}
    for which, core in enumerate((c, 1 - c)):
        device = (2 * me.y + core) * TILES + m
        held = [
            jnp.sum(jnp.where(owner[...] == 2 * device + i, index, 0), axis=(0, 1), keepdims=True)
            for i in range(2)
        ]
        for role, table in tables.items():
            mids, leaves = table[16], table[17]
            entries = []
            for live, block in (
                ((mids >> 2) == device, mids & 3),
                ((leaves == held[0]) | (leaves == held[1]), (leaves == held[1]).astype(jnp.int32)),
            ):
                found = code + block
                first = jnp.min(jnp.where(live, found, BIG), axis=(0, 1), keepdims=True)
                final = jnp.max(jnp.where(live, found, -1), axis=(0, 1), keepdims=True)
                some = first < BIG
                entries.append((some, jnp.where(some, first, 0)))
                two = some & (final != first)
                entries.append((two, jnp.where(two, final, 0)))
            tiles = [(value >> 2) & 15 for _, value in entries]
            spots = jnp.full((1, 128), 4, jnp.int32)
            for e in (3, 2, 1, 0):
                spots = jnp.where(entries[e][0] & (tiles[e] == lane), e, spots)
            at = 32 + 4 * which + role
            planv[at : at + 1, :] = spots
            for e, (valid, value) in enumerate(entries):
                slot = jnp.full((1, 1), e, jnp.int32)
                for f in range(e - 1, -1, -1):
                    slot = jnp.where(entries[f][0] & (tiles[f] == tiles[e]), f, slot)
                slot = jnp.where(valid, slot, e)
                row = jnp.where(lane == 0, jnp.where(valid, value & 3, -1), slot)
                row = jnp.where(lane == 2, tiles[e], row)
                row = jnp.where(lane == 3, value >> 6, row)
                row = jnp.where(lane == 4, (value & 3) + 4 * (e // 2), row)
                at = 16 * which + 4 * role + e
                planv[at : at + 1, :] = row

    owns, sibs = (own0, own1, own2, own3), (sib0, sib1, sib2, sib3)
    tiles_of = (q_own, q_b, q_a, q_2)
    notes_of = (p_own, p_b, p_a, p_2)
    labels = lax.broadcasted_iota(jnp.int32, (BLOCK, TILE), 0)
    for role in range(4):
        owns[role][4] = jnp.zeros((TILE, D), BF16)
        sibs[role][4] = jnp.zeros((TILE, D), BF16)
    slot_sends, slot_notes, term_sends = {}, {}, {}

    def pack(role):
        rows, table = tiles_of[role], notes_of[role]
        group = pl.ds(4 * role, 4)
        for which, slots, notes in ((1, packs, metas), (0, packo, metao)):
            for e in range(4):
                at = 4 * role + e
                tile, cand = plans[16 * which + at, 2], plans[16 * which + at, 3]
                slots[at] = rows[tile]
                level = 4 * (e // 2)
                positives = table[tile][level : level + 4] - BLOCK * cand
                notes[at, 0:4, :] = positives
                notes[at, 4:8, :] = positives
            if which:
                slot_sends[role] = net.send(packs.at[group], packr.at[group], sib)
                slot_notes[role] = net.send(metas.at[group], metar.at[group], sib)
        start_local(packo.at[group], sel.at[0, group])

    def pairs(role, which):
        group = pl.ds(4 * role, 4)
        if which == 0:
            slots, notes, table, out, base = packo, metao, plans, owns[role], 0
        else:
            slot_sends[role].wait_recv()
            slot_notes[role].wait_recv()
            slot_sends[role].wait_send()
            start_local(packr.at[group], sel.at[1, group])
            slots, notes, table, out, base = packr, metar, planrs, packs, 4 * role

        def body(e, carry):
            at = 4 * role + e
            block = vectors[table[at, 4]]
            delta = delta_of(mm(block, slots[at], 1, 1), labels, notes[at])
            held_delta[which, at] = delta
            out[base + e] = mm(delta, block, 0, 0).astype(BF16)
            return carry

        lax.fori_loop(0, 4, body, 0)
        start_local(held_delta.at[which, group], deltas.at[which, group])
        for e in range(3):
            value = out[base + e]
            for f in range(e + 1, 4):
                same = table[4 * role + f, 1] == e
                value += jnp.where(same, out[base + f], jnp.zeros((TILE, D), BF16))
            out[base + e] = value
        if which == 1:
            term_sends[role] = net.send(packs.at[group], sibs[role].at[pl.ds(0, 4)], sib)

    steps = (0, b, a, 2)
    first_axis = ((xa, xb), (za, zb))
    first2, firsta, firstb = {}, {}, {}
    second2, seconda, secondb = {}, {}, {}

    def part(h, role, unit, j):
        tile = me.tile(steps[unit], steps[j]) if h == 0 else me.tile(steps[j], steps[unit])
        cols = slice(h * HALF, (h + 1) * HALF)
        mine = owns[role][plans[32 + role, tile], :, cols]
        return mine + sibs[role][plans[36 + role, tile], :, cols]

    def begin_sum(role):
        term_sends[role].wait_recv()
        for h in range(2):
            for j in range(4):
                s2[h, role, j] = part(h, role, ACROSS, j)
            first2[h, role] = net.send(s2.at[h, role], r2.at[h, role], first_axis[h][0])
        for h in range(2):
            for j in range(4):
                sb[h, role, j] = part(h, role, BACK, j)
            firstb[h, role] = net.send(sb.at[h, role], rb.at[h, role], first_axis[h][1])

    def pass_sum(role):
        for h in range(2):
            first2[h, role].wait_recv()
            for j in range(4):
                r2[h, role, j] = r2[h, role, j] + part(h, role, FRONT, j)
            firsta[h, role] = net.send(r2.at[h, role], ra.at[h, role], first_axis[h][0])

    def begin_second(role):
        for h in range(2):
            firstb[h, role].wait_recv()
            firsta[h, role].wait_recv()
            for j in (ACROSS, BACK, FRONT, OWN):
                rb[h, role, j] = part(h, role, OWN, j) + rb[h, role, j] + ra[h, role, j]
                if j == ACROSS:
                    second2[h, role] = net.send(
                        rb.at[h, role, j], u2.at[h, role], first_axis[1 - h][0]
                    )
                if j == BACK:
                    secondb[h, role] = net.send(
                        rb.at[h, role, j], ub.at[h, role], first_axis[1 - h][1]
                    )

    def pass_second(role):
        for h in range(2):
            second2[h, role].wait_recv()
            u2[h, role] = u2[h, role] + rb[h, role, FRONT]
            seconda[h, role] = net.send(u2.at[h, role], ua.at[h, role], first_axis[1 - h][0])

    def end_second(role):
        for h in range(2):
            secondb[h, role].wait_recv()
            seconda[h, role].wait_recv()
            ub[h, role] = rb[h, role, OWN] + ub[h, role] + ua[h, role]


    to_smem = pltpu.make_async_copy(planv, plans, local_sem.at[len(local)])
    local.append(to_smem)
    to_smem.start()
    plan_send = net.send(planv.at[pl.ds(16, 16)], planr, sib)
    to_smem.wait()
    load_q.wait()
    pack(OWN)
    across_stage(FRONT)
    send_last(ACROSS, OWN)
    forward_last(BACK)
    second_stage(ACROSS)
    bulk_forward(1)
    across_stage(ACROSS)
    for load in load_v:
        load.wait()
    pairs(OWN, 0)
    cx_a.wait_recv()
    pos_row_b = cpall.at[lax.rem(me.x + b, NX)]
    cx_f = net.send(pos_row_b, pos_row_b, xa)
    bulk_forward(2)
    forward_last(FRONT)
    plan_send.wait_recv()
    plan_in = start_local(planr, planrs)
    plan_in.wait()
    pairs(OWN, 1)
    bulk_forward(3)
    forward_last(ACROSS)
    for i in range(4):
        t0_b[i].wait_recv()
    complete(BACK)
    pack(BACK)
    begin_sum(OWN)
    pairs(BACK, 0)
    complete(FRONT)
    pack(FRONT)
    pairs(BACK, 1)
    pass_sum(OWN)
    begin_sum(BACK)
    pairs(FRONT, 0)
    for i in range(4):
        t0_f[i].wait_recv()
    complete(ACROSS)
    pack(ACROSS)
    pairs(FRONT, 1)
    begin_second(OWN)
    pass_sum(BACK)
    begin_sum(FRONT)
    pairs(ACROSS, 0)
    load_c.wait()
    for j in range(8):
        color, role = j // 4, j % 4
        row = (2 * lax.rem(me.y + role_step(color, role), NY) + color) * TILES + m
        start = pl.multiple_of(row * 16, 16)
        cvm[pl.ds(16 * j, 16), :] = cvv[pl.ds(start, 16), :]
    place = lax.broadcasted_iota(jnp.int32, (128, 128), 0)
    chunk = place // 16
    color, role = chunk // 4, lax.rem(chunk, 4)
    step = jnp.where(role == ACROSS, 2, jnp.where(role == FRONT, 1 + 2 * color, 3 - 2 * color))
    step = jnp.where(role == OWN, 0, step)
    owner_grp = 2 * lax.rem(me.y + step, NY) + color
    coarse_ids = (owner_grp * TILES + m) * 16 + lax.rem(place, 16)

    def own_coarse():
        qm = q_own[m]
        total = jnp.zeros((TILE, D), F32)
        for i in range(COARSE // BLOCK):
            vectors = cvv[i * BLOCK : (i + 1) * BLOCK, :]
            labels = lax.broadcasted_iota(jnp.int32, (BLOCK, TILE), 0) + i * BLOCK
            delta = delta_of(mm(vectors, qm, 1, 1), labels, cpall[me.x, me.z])
            total += mm(delta, vectors, 0, 0)
        qc[...] = total

    def rows_coarse(lo, hi):
        def body(t, carry):
            qt = q_own[t]
            delta = delta_of(mm(cvm[...], qt, 1, 1), coarse_ids, cpall[t // NZ, lax.rem(t, NZ)])
            gc[...] += mm(delta, qt, 1, 0)
            return carry

        lax.fori_loop(lo, hi, body, 0)


    gc[...] = jnp.zeros_like(gc)
    pass_second(OWN)
    begin_second(BACK)
    pairs(ACROSS, 1)
    pass_sum(FRONT)
    own_coarse()
    begin_sum(ACROSS)
    end_second(OWN)
    pass_second(BACK)
    cx_b.wait_recv()
    cx_f.wait_recv()
    rows_coarse(0, 8)
    pass_sum(ACROSS)
    begin_second(FRONT)
    rows_coarse(8, 16)
    coarse = net.send(gc.at[pl.ds(64 * (1 - c), 64)], gsib, sib)
    pass_second(FRONT)
    begin_second(ACROSS)
    end_second(BACK)
    third_b = net.send(ub.at[:, BACK], wb, down)
    end_second(FRONT)
    coarse.wait_recv()
    for role in range(4):
        gbuf[role] = gc[pl.ds(64 * c + 16 * role, 16)] + gsib[16 * role : 16 * role + 16]
    coarse2 = net.send(gbuf.at[ACROSS], gbuf.at[5], up)
    coarseb = net.send(gbuf.at[BACK], gbuf.at[6], down)
    pass_second(ACROSS)
    coarse2.wait_recv()
    gbuf[4] = gbuf[FRONT] + gbuf[5]
    coarsea = net.send(gbuf.at[4], gbuf.at[7], up)
    end_second(ACROSS)

    third_2 = net.send(ub.at[:, ACROSS], w2, up)
    coarsea.wait_recv()
    coarseb.wait_recv()
    gco[...] = gbuf[OWN] + gbuf[6] + gbuf[7]
    start_local(planv.at[pl.ds(0, 16)], plan.at[0])
    start_local(planr, plan.at[1])
    third_2.wait_recv()
    w2[...] = w2[...] + ub[:, FRONT]
    third_a = net.send(w2, wa, up)
    third_b.wait_recv()
    third_a.wait_recv()
    for h in range(2):
        cols = slice(h * HALF, (h + 1) * HALF)
        gq[:, cols] = (
            qc[:, cols] + ub[h, OWN].astype(F32) + wb[h].astype(F32) + wa[h].astype(F32)
        )
    waited = [load_q, load_c, to_smem, plan_in] + load_v
    for copy in local:
        if not any(copy is done for done in waited):
            copy.wait()
    for copy in net.made:
        if not any(copy is done for done in slot_sends.values()):
            copy.wait_send()


PLACES = SLOTS + 6


def grads_kernel(
    plan, sel, deltas,
    gm, gl,
    counts, bases, entries, rows, held, acc, row_sem, delta_sem, grad_sem,
):
    stores = [(gm, 0), (gm, 1), (gm, 2), (gm, 3), (gl, 0), (gl, 1)]
    for key in range(6):
        counts[key] = 0

    def key_of(e):
        return plan[e // 16, lax.rem(e, 16), 0] + 4 * lax.rem(e // 2, 2)

    def live(e):
        return plan[e // 16, lax.rem(e, 16), 0] >= 0

    def count(e, carry):
        @pl.when(live(e))
        def _():
            counts[key_of(e)] += 1

        return carry

    lax.fori_loop(0, SLOTS, count, 0)
    base = 0
    for key in range(6):
        bases[key] = base
        n = counts[key]
        base += n + lax.rem(n, 2)
        counts[key] = 0

    def row_copy(e, at):
        return pltpu.make_async_copy(sel.at[e // 16, lax.rem(e, 16)], rows.at[at], row_sem.at[at])

    def delta_copy(e, at):
        return pltpu.make_async_copy(
            deltas.at[e // 16, lax.rem(e, 16)], held.at[at], delta_sem.at[at]
        )

    def register(e, carry):
        @pl.when(live(e))
        def _():
            key = key_of(e)
            n = counts[key]
            at = bases[key] + n
            entries[at] = e
            counts[key] = n + 1
            row_copy(e, at).start()
            delta_copy(e, at).start()

        return carry

    lax.fori_loop(0, SLOTS, register, 0)

    def per_key(key, carry):
        n = counts[key]
        start = bases[key]

        @pl.when(n == 0)
        def _():
            acc[key] = jnp.zeros((BLOCK, D), F32)

        def batch(i, inner):
            at = start + 2 * i
            full = 2 * i + 1 < n
            row_copy(entries[at], at).wait()
            delta_copy(entries[at], at).wait()

            @pl.when(full)
            def _():
                row_copy(entries[at + 1], at + 1).wait()
                delta_copy(entries[at + 1], at + 1).wait()

            @pl.when(jnp.logical_not(full))
            def _():
                rows[at + 1] = jnp.zeros((TILE, D), BF16)
                held[at + 1] = jnp.zeros((BLOCK, TILE), BF16)

            both = rows[pl.ds(at, 2)].reshape(2 * TILE, D)
            delta = jnp.concatenate([held[at], held[at + 1]], axis=1)

            @pl.when(i == 0)
            def _():
                for n_col in range(3):
                    cols = slice(n_col * THIRD, (n_col + 1) * THIRD)
                    acc[key, :, cols] = mm(delta, both[:, cols], 1, 0)

            @pl.when(i != 0)
            def _():
                for n_col in range(3):
                    cols = slice(n_col * THIRD, (n_col + 1) * THIRD)
                    acc[key, :, cols] += mm(delta, both[:, cols], 1, 0)

            return inner

        lax.fori_loop(0, (n + 1) // 2, batch, 0)
        for i, (out, j) in enumerate(stores):

            @pl.when(key == i)
            def _():
                pltpu.make_async_copy(acc.at[i], out.at[j], grad_sem.at[i]).start()

        return carry

    lax.fori_loop(0, 6, per_key, 0)
    for i, (out, j) in enumerate(stores):
        pltpu.make_async_copy(acc.at[i], out.at[j], grad_sem.at[i]).wait()


def vmem():
    return pl.BlockSpec(memory_space=pltpu.VMEM)


def smem():
    return pl.BlockSpec(memory_space=pltpu.SMEM)


def hbm():
    return pl.BlockSpec(memory_space=pl.ANY)


def shape(dims, dtype):
    return jax.ShapeDtypeStruct(dims, dtype)


def shards(
    queries,
    coarse_vectors,
    mid_vectors,
    leaf_vectors,
    coarse_pos,
    mid_pos,
    leaf_pos,
    mid_cand,
    leaf_cand,
    leaf_owner,
):
    dma = pltpu.SemaphoreType.DMA
    mib = 1024 * 1024
    group = pltpu.VMEM((TILES, TILE, D), BF16)
    notes = pltpu.VMEM((18, 8, 128), jnp.int32)
    packed = pltpu.VMEM((16, TILE, D), BF16)
    packed_notes = pltpu.VMEM((16, 8, 128), jnp.int32)
    slots = pltpu.VMEM((5, TILE, D), BF16)
    first = pltpu.VMEM((2, 4, 4, TILE, HALF), BF16)
    second = pltpu.VMEM((2, 4, TILE, HALF), BF16)
    third = pltpu.VMEM((2, TILE, HALF), BF16)
    gq, gco, sel, deltas, plan = pl.pallas_call(
        main_kernel,
        out_shape=(
            shape((TILE, D), F32),
            shape((16, D), F32),
            shape((2, 16, TILE, D), BF16),
            shape((2, 16, BLOCK, TILE), BF16),
            shape((2, 16, 128), jnp.int32),
        ),
        in_specs=[hbm(), vmem(), vmem(), vmem(), vmem(), vmem(), vmem(), hbm(), hbm(), hbm()],
        out_specs=(vmem(), vmem(), hbm(), hbm(), hbm()),
        scratch_shapes=[
            group, group, group, group,
            notes, notes, notes, notes,
            pltpu.VMEM((COARSE, D), BF16),
            pltpu.VMEM((128, D), BF16),
            pltpu.VMEM((NX, NZ, 8, TILE), jnp.int32),
            packed, packed, packed, packed_notes, packed_notes, packed_notes,
            pltpu.VMEM((40, 128), jnp.int32),
            pltpu.VMEM((16, 128), jnp.int32),
            pltpu.SMEM((40, 128), jnp.int32),
            pltpu.SMEM((16, 128), jnp.int32),
            pltpu.VMEM((6, BLOCK, D), BF16),
            pltpu.VMEM((2, 16, BLOCK, TILE), BF16),
            pltpu.VMEM((128, D), F32),
            pltpu.VMEM((TILE, D), F32),
            slots, slots, slots, slots, slots, slots, slots, slots,
            pltpu.VMEM((64, D), F32),
            pltpu.VMEM((8, 16, D), F32),
            first, first, first, first, first,
            second, second, second,
            third, third, third,
            dma((32,)),
            dma((COPIES,)),
            dma((COPIES,)),
        ],
        compiler_params=pltpu.CompilerParams(
            collective_id=0, has_side_effects=True, vmem_limit_bytes=63 * mib
        ),
        name="main",
    )(
        queries.reshape(TILES, TILE, D),
        mid_pos.T,
        leaf_pos.T,
        mid_cand.T,
        leaf_cand.T,
        coarse_pos.T,
        leaf_owner.reshape(2, 128),
        coarse_vectors,
        mid_vectors.reshape(4, BLOCK, D),
        leaf_vectors.reshape(2, BLOCK, D),
    )
    gm, gl = pl.pallas_call(
        grads_kernel,
        out_shape=(shape((4, BLOCK, D), F32), shape((2, BLOCK, D), F32)),
        in_specs=[smem(), hbm(), hbm()],
        out_specs=(hbm(), hbm()),
        scratch_shapes=[
            pltpu.SMEM((6,), jnp.int32),
            pltpu.SMEM((6,), jnp.int32),
            pltpu.SMEM((PLACES,), jnp.int32),
            pltpu.VMEM((PLACES, TILE, D), BF16),
            pltpu.VMEM((PLACES, BLOCK, TILE), BF16),
            pltpu.VMEM((6, BLOCK, D), F32),
            dma((PLACES,)),
            dma((PLACES,)),
            dma((6,)),
        ],
        compiler_params=pltpu.CompilerParams(vmem_limit_bytes=40 * mib),
        name="grads",
    )(plan, sel, deltas)
    return gq, gco, gm.reshape(4 * BLOCK, D), gl.reshape(2 * BLOCK, D)


def solution(mesh):
    placed = (
        P("grp", None),
        P(),
        P(("grp", "mid"), None),
        P(("grp", "mid"), None),
        P(("grp", "mid"), None),
        P("grp", None),
        P("grp", None),
        P("grp", None),
        P("grp", None),
        P(),
    )
    return jax.shard_map(
        shards,
        mesh=mesh,
        in_specs=placed,
        out_specs=(
            P(("grp", "mid"), None),
            P(("grp", "mid"), None),
            P(("grp", "mid"), None),
            P(("grp", "mid"), None),
        ),
        check_vma=False,
    )
```

time: 562 us -> 166 us (0.30)
  waiting for transfers between devices: 294 us -> 0 us
  Pallas kernels: 0 us -> 156 us
  matrix products: 143 us -> 0 us
  local copies, waits for them, and re-layouts: 64.8 us -> 7.06 us
  other arithmetic: 22.4 us -> 0 us
  starting transfers between devices: 19.8 us -> 0 us
  between operations: 14.6 us -> 0.67 us
    reduce_scatter x2 -> x0, waiting for transfers between devices: 174 us -> none  [the longest x1 174 us: shards(): lax.psum_scatter(lax.dot_general(coarse_delta, own_rows, (((0,), (0,)), (...]
    pallas_call x0 -> x2, Pallas kernels: none -> 156 us  [the longest x1 141 us: shards(): pl.pallas_call(main_kernel, out_shape=(shape((TILE, D), F32), shape((16,...]
    dot_general x8 -> x0, matrix products: 143 us -> none  [the longest x1 64 us: shards(): jnp.einsum('gnb,gnld->bld', block_onehot, block_terms, precision=lax.Prec...]
    all_to_all x4 -> x0, waiting for transfers between devices: 119 us -> none  [the longest x1 72.1 us: shards(): lax.all_to_all(query_terms, 'grp', split_axis=0, concat_axis=0, tiled=True)]
    slice x4 -> x0, local copies, waits for them, and re-layouts: 23.5 us -> none  [the longest x2 15.2 us: shards(): grad_mid = block_grads[:mid_blocks].reshape(mid_blocks * BLOCK, feature)]
    gather x11 -> x0, local copies, waits for them, and re-layouts: 20 us -> none  [the longest x1 12.4 us: shards(): vectors = storage[jnp.maximum(request_slot, 0)]]
    all_to_all x4 -> x0, starting transfers between devices: 19.5 us -> none  [the longest x1 5.38 us: shards(): lax.all_to_all(tile_rows, 'grp', split_axis=0, concat_axis=0, tiled=True)]
    concatenate x5 -> x0, other arithmetic: 11.7 us -> none  [the longest x1 6.09 us: shards(): tile_rows = jnp.concatenate([mid_plan[0], leaf_plan[0]], axis=1)]
  transfers between devices with their start and end apart: 6 -> 0, of which waited for: 3 -> 0; matrix products, arithmetic and copies ran while one was open for 29% -> 0% of each run, Pallas kernels for 0% -> 0%
where the time goes in v1:
time: 166 us; the launch traced here: 164 us
  Pallas kernels  156 us (94%)
  local copies, waits for them, and re-layouts  7.06 us (4%)
    pallas_call x1, Pallas kernels, shards(): pl.pallas_call(main_kernel, out_shape=(shape((TILE, D), F32), shape((16,...  141 us
    pallas_call x1, Pallas kernels, shards(): pl.pallas_call(grads_kernel, out_shape=(shape((4, BLOCK, D), F32), shape(...  14.8 us
    unnamed x12, local copies, waits for them, and re-layouts  7.06 us

profile of v1, /device:TPU:0, one launch (start us, length us, event | category | flops | bytes accessed | tf_op | source)
XLA Modules:
  0.0 163.7 jit_solution(8884406716325077804)
XLA Ops:
  0.6 141.2 %main.1 = (f32[128,768]{1,0:T(8,128)}, f32[16,768]{1,0:T(8,128)}, bf16[2,16,128,768]{3,2,1,0:T(8,128)(2,1)}, bf16[2,16,512,128]{3,2,1,0:T(8,128)(2,1)}, s32[2,16,128]{2,1,0:T(8,128)}) custom-call(bf16[16,128,768]{2,1,0:T(8,128)(2,1)} %bitcast.11, s32[4,2048]{1,0:T(4,128)} %bitcast.14, s32[4,2048]{1,0:T(4,128)} %bitcast.15, s32[8,16]{1,0:T(8,128)} %bitcast.16, ...), custom_call_target="tpu_custom_call" | custom-call | tf_op jit(solution)/shard_map/main/pallas_call | solution.py:683
  141.8 0.0 copy-start
  141.8 2.8 %copy-done = bf16[2,16,128,768]{3,2,1,0:T(8,128)(2,1)S(1)} copy-done((bf16[2,16,128,768]{3,2,1,0:T(8,128)(2,1)S(1)}, bf16[2,16,128,768]{3,2,1,0:T(8,128)(2,1)}, u32[]{:S(2)}) %copy-start) | copy-done | bytes 6291480
  144.6 0.0 copy-start.1
  144.6 2.2 %copy-done.1 = bf16[2,16,512,128]{3,2,1,0:T(8,128)(2,1)S(1)} copy-done((bf16[2,16,512,128]{3,2,1,0:T(8,128)(2,1)S(1)}, bf16[2,16,512,128]{3,2,1,0:T(8,128)(2,1)}, u32[]{:S(2)}) %copy-start.1) | copy-done | bytes 4194328
  146.8 0.0 copy-start.2
  146.8 0.7 copy-done.2
  147.5 0.0 copy-start.3
  147.5 0.0 copy-start.4
  147.5 14.8 %grads.1 = (f32[4,512,768]{2,1,0:T(8,128)}, f32[2,512,768]{2,1,0:T(8,128)}) custom-call(s32[2,16,128]{2,1,0:T(8,128)S(1)} %copy-done.2, bf16[2,16,128,768]{3,2,1,0:T(8,128)(2,1)S(1)} %copy-done, bf16[2,16,512,128]{3,2,1,0:T(8,128)(2,1)S(1)} %copy-done.1), custom_call_target="tpu_custom_call" | custom-call | tf_op jit(solution)/shard_map/grads/pallas_call | solution.py:735
  162.3 0.0 copy-done.3
  162.3 0.7 copy.16
  163.0 0.0 copy-done.4
  163.0 0.6 copy.17
Async XLA Ops:
  141.8 2.8 %copy-start = (bf16[2,16,128,768]{3,2,1,0:T(8,128)(2,1)S(1)}, bf16[2,16,128,768]{3,2,1,0:T(8,128)(2,1)}, u32[]{:S(2)}) copy-start(bf16[2,16,128,768]{3,2,1,0:T(8,128)(2,1)} %get-tuple-element.14.sel) | copy-start | bytes 18874372
  144.6 2.2 %copy-start.1 = (bf16[2,16,512,128]{3,2,1,0:T(8,128)(2,1)S(1)}, bf16[2,16,512,128]{3,2,1,0:T(8,128)(2,1)}, u32[]{:S(2)}) copy-start(bf16[2,16,512,128]{3,2,1,0:T(8,128)(2,1)} %get-tuple-element.15.deltas) | copy-start | bytes 12582916
  146.8 0.7 copy-start.2
  147.5 14.8 %copy-start.3 = (f32[128,768]{1,0:T(8,128)S(1)}, f32[128,768]{1,0:T(8,128)}, u32[]{:S(2)}) copy-start(f32[128,768]{1,0:T(8,128)} %get-tuple-element.22) | copy-start | bytes 1179652
  147.5 15.5 %copy-start.4 = (f32[16,768]{1,0:T(8,128)S(1)}, f32[16,768]{1,0:T(8,128)}, u32[]{:S(2)}) copy-start(f32[16,768]{1,0:T(8,128)} %get-tuple-element.23) | copy-start | bytes 147460

commit v2 on v1

v2 whole, which is shorter than its diff:
```python
import jax
import jax.numpy as jnp
from jax import lax
from jax.experimental import pallas as pl
from jax.experimental.pallas import tpu as pltpu
from jax.sharding import PartitionSpec as P

TILE = 128
BLOCK = 512
COARSE = 2048
K_CAND = 8
D = 768
NY, NX, NZ = 4, 4, 4
TILES = NX * NZ
BIG = 1 << 20
F32 = jnp.float32
BF16 = jnp.bfloat16
MESH = pl.DeviceIdType.MESH
R0, R1, R2 = (0, 32), (32, 48), (80, 48)
ROWS0, ROWS1, ROWS2 = pl.ds(*R0), pl.ds(*R1), pl.ds(*R2)
THIRD = D // 3


def mm(a, b, ca, cb):
    return lax.dot_general(a, b, (((ca,), (cb,)), ((), ())), preferred_element_type=F32)


def delta_of(scores, labels, positives):
    hit = labels == positives[0:1]
    for p in range(1, 4):
        hit = hit | (labels == positives[p : p + 1])
    return (0.125 * jnp.tanh(0.5 * scores) + jnp.where(hit, -0.125, 0.125)).astype(BF16)


class Place:
    def __init__(self):
        grp, mid = lax.axis_index("grp"), lax.axis_index("mid")
        self.y, self.c = grp // 2, lax.rem(grp, 2)
        self.x, self.z = mid // NZ, lax.rem(mid, NZ)
        self.mid = mid
        self.ahead = 1 + 2 * self.c
        self.behind = 3 - 2 * self.c

    def at(self, dy=0, dx=0, dz=0):
        y, x, z = lax.rem(self.y + dy, NY), lax.rem(self.x + dx, NX), lax.rem(self.z + dz, NZ)
        return (2 * y + self.c, NZ * x + z)

    def sibling(self):
        return (2 * self.y + 1 - self.c, self.mid)

    def tile(self, dx, dz):
        return NZ * lax.rem(self.x + dx, NX) + lax.rem(self.z + dz, NZ)

    def greet(self):
        near = [self.sibling()]
        for step in (self.ahead, self.behind):
            near += [self.at(dy=step), self.at(dx=step), self.at(dz=step)]
        barrier = pltpu.get_barrier_semaphore()
        for device in near:
            pl.semaphore_signal(barrier, inc=1, device_id=device, device_id_type=MESH)
        pl.semaphore_wait(barrier, len(near))


class Net:
    def __init__(self, send_sem, recv_sem):
        self.send_sem, self.recv_sem, self.made = send_sem, recv_sem, []

    def send(self, src, dst, device):
        i = len(self.made)
        copy = pltpu.make_async_remote_copy(
            src_ref=src,
            dst_ref=dst,
            send_sem=self.send_sem.at[i],
            recv_sem=self.recv_sem.at[i],
            device_id=device,
            device_id_type=MESH,
        )
        copy.start()
        self.made.append(copy)
        return copy

    def finish(self):
        for copy in self.made:
            copy.wait_send()


GATHER_COPIES = 128
OWN, BACK, FRONT, ACROSS = range(4)


def role_step(color, role):
    return (0, 3 - 2 * color, 1 + 2 * color, 2)[role]


def gather_kernel(
    q, mp, lp, mc, lc, cp, owner, cv,
    sel, meta, plan, tbl, gc, qc,
    q_own, q_b, q_a, q_2, p_own, p_b, p_a, p_2, cvv, cvm, cpall, packo, packs, metao, metas,
    planv, plans, local_sem, send_sem, recv_sem,
):
    me = Place()
    c, a, b = me.c, me.ahead, me.behind
    net = Net(send_sem, recv_sem)
    loads = [
        pltpu.make_async_copy(q, q_own, local_sem.at[0]),
        pltpu.make_async_copy(cv, cvv, local_sem.at[1]),
    ]
    for load in loads:
        load.start()
    for t in range(TILES):
        p_own[t, 0:4, :] = mp[:, t * TILE : (t + 1) * TILE]
        p_own[t, 4:8, :] = lp[:, t * TILE : (t + 1) * TILE]
    p_own[16:18] = jnp.full((2, 8, 128), -1, jnp.int32)
    p_own[16, :, 0:TILES] = mc[...]
    p_own[17, :, 0:TILES] = lc[...]
    cpall[me.x, me.z, 0:4, :] = cp[...]
    cpall[me.x, me.z, 4:8, :] = cp[...]
    me.greet()

    m = me.mid
    small = pl.ds(R1[0], R1[1] + R2[1])
    up, down = me.at(dy=a), me.at(dy=b)
    xa, xb, za, zb = me.at(dx=a), me.at(dx=b), me.at(dz=a), me.at(dz=b)
    sib = me.sibling()
    planes = {BACK: q_b, FRONT: q_a, ACROSS: q_2}

    y_a = net.send(q.at[m, small], q_b.at[m, small], up)
    y_b = net.send(q.at[m, small], q_a.at[m, small], down)
    at_y = {BACK: y_a, FRONT: y_b}
    pos_own = cpall.at[me.x, me.z]
    cz_a = net.send(pos_own, pos_own, za)
    cz_b = net.send(pos_own, pos_own, zb)
    pr_a = net.send(p_own, p_b, up)
    pr_b = net.send(p_own, p_a, down)

    def bulk(i):
        return pl.ds(4 * i, 4)

    t0_a, t0_b, t0_f = [], [], []

    def bulk_own(i):
        t0_a.append(net.send(q.at[bulk(i), ROWS0], q_b.at[bulk(i), ROWS0], up))
        t0_b.append(net.send(q.at[bulk(i), ROWS0], q_a.at[bulk(i), ROWS0], down))

    def bulk_forward(i):
        t0_a[i].wait_recv()
        t0_f.append(net.send(q_b.at[bulk(i), ROWS0], q_2.at[bulk(i), ROWS0], up))

    bulk_own(0)

    axes = ((ROWS1, za, zb, xa, xb), (ROWS2, xa, xb, za, zb))

    def tile_of(h, first, last):
        return me.tile(last, first) if h == 0 else me.tile(first, last)

    second, second_f, last, last_f = {}, {}, {}, {}
    walk = (0, b, a, 2)

    def send_second(role):
        for h, (rows, to_a, to_b, _, _) in enumerate(axes):
            piece = planes[role].at[m, rows]
            second[role, h] = (net.send(piece, piece, to_a), net.send(piece, piece, to_b))

    def send_last(role, key):
        step = walk[key]
        for h, (rows, _, _, to_a, to_b) in enumerate(axes):
            piece = planes[role].at[tile_of(h, step, 0), rows]
            last[role, h, key] = (net.send(piece, piece, to_a), net.send(piece, piece, to_b))

    def second_stage(role):
        for h, (rows, to_a, _, _, _) in enumerate(axes):
            second[role, h][0].wait_recv()
            piece = planes[role].at[tile_of(h, b, 0), rows]
            second_f[role, h] = net.send(piece, piece, to_a)
        send_last(role, BACK)
        for h in range(2):
            second[role, h][1].wait_recv()
        send_last(role, FRONT)

    def across_stage(role):
        for h in range(2):
            second_f[role, h].wait_recv()
        send_last(role, ACROSS)

    def forward_last(role):
        for key, step in enumerate(walk):
            for h, (rows, _, _, to_a, _) in enumerate(axes):
                last[role, h, key][0].wait_recv()
                piece = planes[role].at[tile_of(h, step, b), rows]
                last_f[role, h, key] = net.send(piece, piece, to_a)

    def complete(role):
        for key in range(4):
            for h in range(2):
                last[role, h, key][1].wait_recv()
                last_f[role, h, key].wait_recv()

    y_a.wait_recv()
    y_f = net.send(q_b.at[m, small], q_2.at[m, small], up)
    send_second(BACK)
    y_b.wait_recv()
    send_second(FRONT)
    cz_a.wait_recv()
    pos_b = cpall.at[me.x, lax.rem(me.z + b, NZ)]
    cz_f = net.send(pos_b, pos_b, za)
    pr_a.wait_recv()
    pr_f = net.send(p_b, p_2, up)
    bulk_own(1)
    send_last(BACK, OWN)
    second_stage(BACK)
    y_f.wait_recv()
    send_second(ACROSS)
    bulk_own(2)
    bulk_own(3)
    across_stage(BACK)
    send_last(FRONT, OWN)
    second_stage(FRONT)
    cz_b.wait_recv()
    cz_f.wait_recv()
    pos_row = cpall.at[me.x]
    cx_a = net.send(pos_row, pos_row, xa)
    cx_b = net.send(pos_row, pos_row, xb)
    bulk_forward(0)
    across_stage(FRONT)
    send_last(ACROSS, OWN)
    forward_last(BACK)
    second_stage(ACROSS)
    bulk_forward(1)
    across_stage(ACROSS)
    bulk_forward(2)
    forward_last(FRONT)
    bulk_forward(3)

    pr_b.wait_recv()
    pr_f.wait_recv()
    index = lax.broadcasted_iota(jnp.int32, (2, 128), 0) * 128 + lax.broadcasted_iota(
        jnp.int32, (2, 128), 1
    )
    code = 4 * (
        TILES * lax.broadcasted_iota(jnp.int32, (8, 128), 0)
        + lax.broadcasted_iota(jnp.int32, (8, 128), 1)
    )
    lane = lax.broadcasted_iota(jnp.int32, (1, 128), 1)
    tables = {OWN: p_own, BACK: p_b, FRONT: p_a, ACROSS: p_2}
    for which, core in enumerate((c, 1 - c)):
        device = (2 * me.y + core) * TILES + m
        held = [
            jnp.sum(jnp.where(owner[...] == 2 * device + i, index, 0), axis=(0, 1), keepdims=True)
            for i in range(2)
        ]
        for role, table in tables.items():
            mids, leaves = table[16], table[17]
            entries = []
            for live, block in (
                ((mids >> 2) == device, mids & 3),
                ((leaves == held[0]) | (leaves == held[1]), (leaves == held[1]).astype(jnp.int32)),
            ):
                found = code + block
                first = jnp.min(jnp.where(live, found, BIG), axis=(0, 1), keepdims=True)
                final = jnp.max(jnp.where(live, found, -1), axis=(0, 1), keepdims=True)
                some = first < BIG
                entries.append((some, jnp.where(some, first, 0)))
                two = some & (final != first)
                entries.append((two, jnp.where(two, final, 0)))
            tiles = [(value >> 2) & 15 for _, value in entries]
            spots = jnp.full((1, 128), 4, jnp.int32)
            for e in (3, 2, 1, 0):
                spots = jnp.where(entries[e][0] & (tiles[e] == lane), e, spots)
            tbl[4 * which + role : 4 * which + role + 1, :] = spots
            for e, (valid, value) in enumerate(entries):
                slot = jnp.full((1, 1), e, jnp.int32)
                alone = jnp.full((1, 1), 1, jnp.int32)
                for f in range(3, -1, -1):
                    if f != e:
                        same = valid & entries[f][0] & (tiles[f] == tiles[e])
                        alone = jnp.where(same, 0, alone)
                        if f < e:
                            slot = jnp.where(same, f, slot)
                row = jnp.where(lane == 0, jnp.where(valid, value & 3, -1), slot + 4 * role)
                row = jnp.where(lane == 2, tiles[e], row)
                row = jnp.where(lane == 3, value >> 6, row)
                row = jnp.where(lane == 4, alone, row)
                at = 16 * which + 4 * role + e
                planv[at : at + 1, :] = row
    to_smem = pltpu.make_async_copy(planv, plans, local_sem.at[2])
    to_smem.start()
    for load in loads:
        load.wait()
    to_smem.wait()
    stored = [pltpu.make_async_copy(planv.at[pl.ds(0, 16)], plan.at[c], local_sem.at[3])]
    stored[0].start()
    arrivals = [net.send(planv.at[pl.ds(16, 16)], plan.at[c], sib)]

    def pack(role, rows, table):
        for which, (slots, notes) in enumerate(((packo, metao), (packs, metas))):
            for e in range(4):
                at = 4 * role + e
                tile, cand = plans[16 * which + at, 2], plans[16 * which + at, 3]
                slots[at] = rows[tile]
                level = 4 * (e // 2)
                positives = table[tile][level : level + 4] - BLOCK * cand
                notes[at, 0:4, :] = positives
                notes[at, 4:8, :] = positives
        group = pl.ds(4 * role, 4)
        arrivals.append(net.send(packs.at[group], sel.at[c, group], sib))
        own = pltpu.make_async_copy(packo.at[group], sel.at[c, group], local_sem.at[4 + role])
        own.start()
        stored.append(own)

    pack(OWN, q_own, p_own)
    cx_a.wait_recv()
    pos_row_b = cpall.at[lax.rem(me.x + b, NX)]
    cx_f = net.send(pos_row_b, pos_row_b, xa)
    forward_last(ACROSS)

    for j in range(8):
        color, role = j // 4, j % 4
        row = (2 * lax.rem(me.y + role_step(color, role), NY) + color) * TILES + m
        start = pl.multiple_of(row * 16, 16)
        cvm[pl.ds(16 * j, 16), :] = cvv[pl.ds(start, 16), :]
    place = lax.broadcasted_iota(jnp.int32, (128, 128), 0)
    chunk = place // 16
    color, role = chunk // 4, lax.rem(chunk, 4)
    step = jnp.where(role == ACROSS, 2, jnp.where(role == FRONT, 1 + 2 * color, 3 - 2 * color))
    step = jnp.where(role == OWN, 0, step)
    owner_grp = 2 * lax.rem(me.y + step, NY) + color
    coarse_ids = (owner_grp * TILES + m) * 16 + lax.rem(place, 16)

    def own_coarse():
        qm = q_own[m]
        total = jnp.zeros((TILE, D), F32)
        for i in range(COARSE // BLOCK):
            vectors = cvv[i * BLOCK : (i + 1) * BLOCK, :]
            labels = lax.broadcasted_iota(jnp.int32, (BLOCK, TILE), 0) + i * BLOCK
            delta = delta_of(mm(vectors, qm, 1, 1), labels, cpall[me.x, me.z])
            total += mm(delta, vectors, 0, 0)
        qc[...] = total

    def rows_coarse(lo, hi):
        def body(t, carry):
            qt = q_own[t]
            delta = delta_of(mm(cvm[...], qt, 1, 1), coarse_ids, cpall[t // NZ, lax.rem(t, NZ)])
            gc[...] += mm(delta, qt, 1, 0)
            return carry

        lax.fori_loop(lo, hi, body, 0)

    gc[...] = jnp.zeros_like(gc)
    for i in range(4):
        t0_b[i].wait_recv()
    complete(BACK)
    pack(BACK, q_b, p_b)
    own_coarse()
    complete(FRONT)
    pack(FRONT, q_a, p_a)
    cx_b.wait_recv()
    cx_f.wait_recv()
    rows_coarse(0, 8)
    for i in range(4):
        t0_f[i].wait_recv()
    complete(ACROSS)
    pack(ACROSS, q_2, p_2)
    arrivals.append(net.send(metas, meta.at[c], sib))
    notes = pltpu.make_async_copy(metao, meta.at[c], local_sem.at[8])
    notes.start()
    stored.append(notes)
    rows_coarse(8, 16)
    for copy in stored:
        copy.wait()
    for copy in arrivals:
        copy.wait_recv()
    net.finish()


SLOTS = 32
LIST = 16


def local_kernel(
    plan, meta, midv, leafv, sel,
    gm, gl, qt,
    counts, entries, begun, rows, vectors, acc, terms, row_sem, vec_sem, grad_sem, term_sem,
):
    stores = [(gm, 0), (gm, 1), (gm, 2), (gm, 3), (gl, 0), (gl, 1)]

    def row_copy(e):
        return pltpu.make_async_copy(sel.at[e], rows.at[e], row_sem.at[e])

    def term_copy(e):
        return pltpu.make_async_copy(terms.at[e], qt.at[e], term_sem.at[e])

    for key in range(6):
        counts[key] = 0
    for e in range(SLOTS):
        block = plan[e, 0]
        begun[e] = 0

        @pl.when(block >= 0)
        def _():
            row_copy(e).start()
            key = block + 4 * (e // 2 % 2)
            n = counts[key]
            entries[LIST * key + n] = e
            counts[key] = n + 1

    for key, (src, i) in enumerate([(midv, i) for i in range(4)] + [(leafv, i) for i in range(2)]):
        pltpu.make_async_copy(src.at[i], vectors.at[key], vec_sem.at[key]).start()
    rows[SLOTS] = jnp.zeros((TILE, D), BF16)
    labels = lax.broadcasted_iota(jnp.int32, (BLOCK, TILE), 0)

    def put(e, value):
        slot = (e & 16) + plan[e, 1]

        @pl.when(begun[slot] == 0)
        def _():
            terms[slot] = value.astype(BF16)

        @pl.when(begun[slot] != 0)
        def _():
            terms[slot] = (terms[slot].astype(F32) + value).astype(BF16)

        begun[slot] = 1

        @pl.when(plan[e, 4] == 1)
        def _():
            term_copy(e).start()

    def per_key(key, carry):
        n = counts[key]
        start = LIST * key
        pltpu.make_async_copy(leafv.at[0], vectors.at[key], vec_sem.at[key]).wait()

        @pl.when(n == 0)
        def _():
            acc[key] = jnp.zeros((BLOCK, D), F32)

        def batch(i, inner):
            at = start + 2 * i
            full = 2 * i + 1 < n
            e0 = entries[at]
            e1 = jnp.where(full, entries[at + 1], SLOTS)
            row_copy(e0).wait()

            @pl.when(full)
            def _():
                row_copy(e1).wait()

            block = vectors[key]
            both = jnp.concatenate([rows[e0], rows[e1]], axis=0)
            scores = mm(block, both, 1, 1)
            delta = jnp.concatenate(
                [
                    delta_of(scores[:, 0:TILE], labels, meta[e0]),
                    delta_of(scores[:, TILE : 2 * TILE], labels, meta[jnp.minimum(e1, SLOTS - 1)]),
                ],
                axis=1,
            )

            @pl.when(i == 0)
            def _():
                for n_col in range(3):
                    cols = slice(n_col * THIRD, (n_col + 1) * THIRD)
                    acc[key, :, cols] = mm(delta, both[:, cols], 1, 0)

            @pl.when(i != 0)
            def _():
                for n_col in range(3):
                    cols = slice(n_col * THIRD, (n_col + 1) * THIRD)
                    acc[key, :, cols] += mm(delta, both[:, cols], 1, 0)

            term = mm(delta, block, 0, 0)
            put(e0, term[0:TILE])

            @pl.when(full)
            def _():
                put(e1, term[TILE : 2 * TILE])

            return inner

        lax.fori_loop(0, (n + 1) // 2, batch, 0)
        for i, (out, j) in enumerate(stores):

            @pl.when(key == i)
            def _():
                pltpu.make_async_copy(acc.at[i], out.at[j], grad_sem.at[i]).start()

        return carry

    lax.fori_loop(0, 6, per_key, 0)
    for e in range(SLOTS):

        @pl.when((plan[e, 0] >= 0) & (plan[e, 4] == 0) & (begun[e] != 0))
        def _():
            term_copy(e).start()

    for e in range(SLOTS):

        @pl.when(begun[e] != 0)
        def _():
            term_copy(e).wait()

    for i, (out, j) in enumerate(stores):
        pltpu.make_async_copy(acc.at[i], out.at[j], grad_sem.at[i]).wait()


SCATTER_COPIES = 80


def scatter_kernel(
    tbl, qt, gcp, qc,
    gq, gco,
    own0, own1, own2, own3, sib0, sib1, sib2, sib3, gsib, gbuf,
    s2, sb, r2, rb, ra, u2, ub, ua, w2, wb, wa, local_sem, send_sem, recv_sem,
):
    me = Place()
    c, a, b = me.c, me.ahead, me.behind
    far = 1 - c
    net = Net(send_sem, recv_sem)
    owns, sibs = (own0, own1, own2, own3), (sib0, sib1, sib2, sib3)
    order = (ACROSS, BACK, FRONT, OWN)
    loads = {}
    for role in order:
        loads[role] = pltpu.make_async_copy(
            qt.at[c, pl.ds(4 * role, 4)], owns[role].at[pl.ds(0, 4)], local_sem.at[role]
        )
        loads[role].start()
    for role in order:
        owns[role][4] = jnp.zeros((TILE, D), BF16)
        sibs[role][4] = jnp.zeros((TILE, D), BF16)
    me.greet()
    sib = me.sibling()
    halves = {}
    for role in order:
        halves[role] = net.send(
            qt.at[far, pl.ds(4 * role, 4)], sibs[role].at[pl.ds(0, 4)], sib
        )
    coarse = net.send(gcp.at[far], gsib.at[pl.ds(0, 4)], sib)
    ahead = [me.at(dy=a), me.at(dx=a), me.at(dz=a)]
    behind = [me.at(dy=b), me.at(dx=b), me.at(dz=b)]
    steps = (0, b, a, 2)
    orders = ((0, 1, 2), (1, 2, 0), (2, 0, 1))

    def chunk(k, *units):
        at = [0, 0, 0]
        for axis, unit in zip(orders[k], units):
            at[axis] = unit
        role, tile = at[0], me.tile(steps[at[1]], steps[at[2]])
        cols = slice(k * THIRD, (k + 1) * THIRD)
        return owns[role][tbl[role, tile], :, cols] + sibs[role][tbl[4 + role, tile], :, cols]

    first2, firsta, firstb = {}, {}, {}

    def start2(k, i):
        for j in range(4):
            s2[k, i, j] = chunk(k, ACROSS, i, j)
        first2[k, i] = net.send(s2.at[k, i], r2.at[k, i], ahead[orders[k][0]])

    def startb(k, i):
        for j in range(4):
            sb[k, i, j] = chunk(k, BACK, i, j)
        firstb[k, i] = net.send(sb.at[k, i], rb.at[k, i], behind[orders[k][0]])

    def starta(k, i):
        first2[k, i].wait_recv()
        for j in range(4):
            r2[k, i, j] = r2[k, i, j] + chunk(k, FRONT, i, j)
        firsta[k, i] = net.send(r2.at[k, i], ra.at[k, i], ahead[orders[k][0]])

    def arrive(role):
        loads[role].wait()
        halves[role].wait_recv()

    arrive(ACROSS)
    for i in order:
        start2(0, i)
    arrive(BACK)
    for i in order:
        startb(0, i)
    arrive(FRONT)
    arrive(OWN)
    for i in order:
        for k in (1, 2):
            start2(k, i)
            startb(k, i)

    coarse.wait_recv()
    for role in range(4):
        gbuf[role] = gcp[c, role] + gsib[role]
    coarse2 = net.send(gbuf.at[ACROSS], gsib.at[4], ahead[0])
    coarseb = net.send(gbuf.at[BACK], gsib.at[5], behind[0])
    for i in order:
        for k in range(3):
            starta(k, i)
    coarse2.wait_recv()
    gbuf[4] = gbuf[FRONT] + gsib[4]
    coarsea = net.send(gbuf.at[4], gsib.at[6], ahead[0])

    second2, seconda, secondb = {}, {}, {}
    for i in order:
        for k in range(3):
            firstb[k, i].wait_recv()
            firsta[k, i].wait_recv()
            for j in range(4):
                rb[k, i, j] = chunk(k, OWN, i, j) + rb[k, i, j] + ra[k, i, j]
            if i == ACROSS:
                second2[k] = net.send(rb.at[k, i], u2.at[k], ahead[orders[k][1]])
            if i == BACK:
                secondb[k] = net.send(rb.at[k, i], ub.at[k], behind[orders[k][1]])
            if i == FRONT:
                second2[k].wait_recv()
                u2[k] = u2[k] + rb[k, i]
                seconda[k] = net.send(u2.at[k], ua.at[k], ahead[orders[k][1]])
    coarsea.wait_recv()
    coarseb.wait_recv()
    gco[...] = gbuf[OWN] + gsib[5] + gsib[6]

    third2, thirda, thirdb = [], [], []
    for k in range(3):
        secondb[k].wait_recv()
        seconda[k].wait_recv()
        ub[k] = rb[k, OWN] + ub[k] + ua[k]
        third2.append(net.send(ub.at[k, ACROSS], w2.at[k], ahead[orders[k][2]]))
        thirdb.append(net.send(ub.at[k, BACK], wb.at[k], behind[orders[k][2]]))
    for k in range(3):
        third2[k].wait_recv()
        w2[k] = w2[k] + ub[k, FRONT]
        thirda.append(net.send(w2.at[k], wa.at[k], ahead[orders[k][2]]))
    for k in range(3):
        thirdb[k].wait_recv()
        thirda[k].wait_recv()
        cols = slice(k * THIRD, (k + 1) * THIRD)
        gq[:, cols] = (
            qc[:, cols] + ub[k, OWN].astype(F32) + wb[k].astype(F32) + wa[k].astype(F32)
        )
    net.finish()


def vmem():
    return pl.BlockSpec(memory_space=pltpu.VMEM)


def smem():
    return pl.BlockSpec(memory_space=pltpu.SMEM)


def hbm():
    return pl.BlockSpec(memory_space=pl.ANY)


def shape(dims, dtype):
    return jax.ShapeDtypeStruct(dims, dtype)


def shards(
    queries,
    coarse_vectors,
    mid_vectors,
    leaf_vectors,
    coarse_pos,
    mid_pos,
    leaf_pos,
    mid_cand,
    leaf_cand,
    leaf_owner,
):
    dma = pltpu.SemaphoreType.DMA
    limit = 56 * 1024 * 1024
    group = pltpu.VMEM((TILES, TILE, D), BF16)
    notes = pltpu.VMEM((18, 8, 128), jnp.int32)
    packed = pltpu.VMEM((16, TILE, D), BF16)
    packed_notes = pltpu.VMEM((16, 8, 128), jnp.int32)
    sel, meta, plan, tbl, gc, qc = pl.pallas_call(
        gather_kernel,
        out_shape=(
            shape((2, 16, TILE, D), BF16),
            shape((2, 16, 8, 128), jnp.int32),
            shape((2, 16, 128), jnp.int32),
            shape((8, 128), jnp.int32),
            shape((128, D), F32),
            shape((TILE, D), F32),
        ),
        in_specs=[hbm(), vmem(), vmem(), vmem(), vmem(), vmem(), vmem(), hbm()],
        out_specs=(hbm(), hbm(), hbm(), vmem(), vmem(), vmem()),
        scratch_shapes=[
            group, group, group, group,
            notes, notes, notes, notes,
            pltpu.VMEM((COARSE, D), BF16),
            pltpu.VMEM((128, D), BF16),
            pltpu.VMEM((NX, NZ, 8, TILE), jnp.int32),
            packed, packed, packed_notes, packed_notes,
            pltpu.VMEM((32, 128), jnp.int32),
            pltpu.SMEM((32, 128), jnp.int32),
            dma((9,)),
            dma((GATHER_COPIES,)),
            dma((GATHER_COPIES,)),
        ],
        compiler_params=pltpu.CompilerParams(
            collective_id=0, has_side_effects=True, vmem_limit_bytes=limit
        ),
        name="gather",
    )(
        queries.reshape(TILES, TILE, D),
        mid_pos.T,
        leaf_pos.T,
        mid_cand.T,
        leaf_cand.T,
        coarse_pos.T,
        leaf_owner.reshape(2, 128),
        coarse_vectors,
    )
    gm, gl, qt = pl.pallas_call(
        local_kernel,
        out_shape=(
            shape((4, BLOCK, D), F32),
            shape((2, BLOCK, D), F32),
            shape((SLOTS, TILE, D), BF16),
        ),
        in_specs=[smem(), vmem(), hbm(), hbm(), hbm()],
        out_specs=(hbm(), hbm(), hbm()),
        scratch_shapes=[
            pltpu.SMEM((6,), jnp.int32),
            pltpu.SMEM((6 * LIST + 1,), jnp.int32),
            pltpu.SMEM((SLOTS,), jnp.int32),
            pltpu.VMEM((SLOTS + 1, TILE, D), BF16),
            pltpu.VMEM((6, BLOCK, D), BF16),
            pltpu.VMEM((6, BLOCK, D), F32),
            pltpu.VMEM((SLOTS, TILE, D), BF16),
            dma((SLOTS,)),
            dma((6,)),
            dma((6,)),
            dma((SLOTS,)),
        ],
        compiler_params=pltpu.CompilerParams(vmem_limit_bytes=limit),
        name="pairs",
    )(
        plan.reshape(SLOTS, 128),
        meta.reshape(SLOTS, 8, 128),
        mid_vectors.reshape(4, BLOCK, D),
        leaf_vectors.reshape(2, BLOCK, D),
        sel.reshape(SLOTS, TILE, D),
    )
    slots = pltpu.VMEM((5, TILE, D), BF16)
    first = pltpu.VMEM((3, 4, 4, TILE, THIRD), BF16)
    second = pltpu.VMEM((3, 4, TILE, THIRD), BF16)
    third = pltpu.VMEM((3, TILE, THIRD), BF16)
    gq, gco = pl.pallas_call(
        scatter_kernel,
        out_shape=(shape((TILE, D), F32), shape((16, D), F32)),
        in_specs=[smem(), hbm(), vmem(), vmem()],
        out_specs=(vmem(), vmem()),
        scratch_shapes=[
            slots, slots, slots, slots, slots, slots, slots, slots,
            pltpu.VMEM((7, 16, D), F32),
            pltpu.VMEM((5, 16, D), F32),
            first, first, first, first, first,
            second, second, second,
            third, third, third,
            dma((4,)),
            dma((SCATTER_COPIES,)),
            dma((SCATTER_COPIES,)),
        ],
        compiler_params=pltpu.CompilerParams(
            collective_id=1, has_side_effects=True, vmem_limit_bytes=limit
        ),
        name="scatter",
    )(tbl, qt.reshape(2, 16, TILE, D), gc.reshape(2, NY, 16, D), qc)
    return gq, gco, gm.reshape(4 * BLOCK, D), gl.reshape(2 * BLOCK, D)


def solution(mesh):
    placed = (
        P("grp", None),
        P(),
        P(("grp", "mid"), None),
        P(("grp", "mid"), None),
        P(("grp", "mid"), None),
        P("grp", None),
        P("grp", None),
        P("grp", None),
        P("grp", None),
        P(),
    )
    return jax.shard_map(
        shards,
        mesh=mesh,
        in_specs=placed,
        out_specs=(
            P(("grp", "mid"), None),
            P(("grp", "mid"), None),
            P(("grp", "mid"), None),
            P(("grp", "mid"), None),
        ),
        check_vma=False,
    )
```

time: 166 us -> 155 us (0.934); the launches traced: 164 us -> 155 us
  Pallas kernels: 156 us -> 151 us
  local copies, waits for them, and re-layouts: 7.06 us -> 3.19 us
    pallas_call x2 -> x3, Pallas kernels: 156 us -> 151 us  [the longest x1 75.3 us: shards(): pl.pallas_call(scatter_kernel, out_shape=(shape((TILE, D), F32), shape((1...]
    unnamed x12 -> x2, local copies, waits for them, and re-layouts: 7.06 us -> 3.19 us
where the time goes in v2:
time: 155 us
  Pallas kernels  151 us (97%)
  local copies, waits for them, and re-layouts  3.19 us (2%)
    pallas_call x1, Pallas kernels, shards(): pl.pallas_call(scatter_kernel, out_shape=(shape((TILE, D), F32), shape((1...  75.3 us
    pallas_call x1, Pallas kernels, shards(): pl.pallas_call(gather_kernel, out_shape=(shape((2, 16, TILE, D), BF16), s...  59 us
    pallas_call x1, Pallas kernels, shards(): pl.pallas_call(local_kernel, out_shape=(shape((4, BLOCK, D), F32), shape(...  16.9 us
    unnamed x2, local copies, waits for them, and re-layouts  3.19 us

profile of v2, /device:TPU:0, one launch (start us, length us, event | category | flops | bytes accessed | tf_op | source)
XLA Modules:
  0.0 155.1 jit_solution(7429303128819339212)
XLA Ops:
  0.6 59.0 %gather.1 = (bf16[2,16,128,768]{3,2,1,0:T(8,128)(2,1)}, s32[2,16,8,128]{3,2,1,0:T(8,128)}, s32[2,16,128]{2,1,0:T(8,128)}, s32[8,128]{1,0:T(8,128)}, f32[128,768]{1,0:T(8,128)}, /*index=5*/f32[128,768]{1,0:T(8,128)}) custom-call(bf16[16,128,768]{2,1,0:T(8,128)(2,1)} %bitcast.18, s32[4,2048]{1,0:T(4,128)} %bitcast.23, s32[4,2048]{1,0:T(4,128)} %bitcast.24, ...), custom_call_target="tpu_custom_call" | custom-call | tf_op jit(solution)/shard_map/gather/pallas_call | solution.py:672
  59.6 16.9 %pairs.1 = (f32[4,512,768]{2,1,0:T(8,128)}, f32[2,512,768]{2,1,0:T(8,128)}, bf16[32,128,768]{2,1,0:T(8,128)(2,1)}) custom-call(s32[32,128]{1,0:T(8,128)} %bitcast.25, s32[32,8,128]{2,1,0:T(8,128)} %bitcast.22, bf16[4,512,768]{2,1,0:T(8,128)(2,1)} %bitcast.19, bf16[2,512,768]{2,1,0:T(8,128)(2,1)} %bitcast.20, bf16[32,128,768]{2,1,0:T(8,128)(2,1)} %bitcast.17), custom_call_target="tpu_custom_call" | custom-call | tf_op jit(solution)/shard_map/pairs/pallas_call | solution.py:711
  76.6 75.3 %scatter.1 = (f32[128,768]{1,0:T(8,128)}, f32[16,768]{1,0:T(8,128)}) custom-call(s32[8,128]{1,0:T(8,128)} %get-tuple-element.15.tbl, bf16[2,16,128,768]{3,2,1,0:T(8,128)(2,1)} %bitcast.16, f32[2,4,16,768]{3,2,1,0:T(8,128)} %bitcast.21, f32[128,768]{1,0:T(8,128)} %get-tuple-element.21.qc), custom_call_target="tpu_custom_call" | custom-call | tf_op jit(solution)/shard_map/scatter/pallas_call | solution.py:746
  151.9 1.8 %copy.16 = f32[128,768]{1,0:T(8,128)} copy(f32[128,768]{1,0:T(8,128)} %get-tuple-element.30) | data formatting | bytes 786432
  153.7 1.4 copy.17

commit v3 on v1

v3 whole, which is shorter than its diff:
```python
import jax
import jax.numpy as jnp
from jax import lax
from jax.experimental import pallas as pl
from jax.experimental.pallas import tpu as pltpu
from jax.sharding import PartitionSpec as P

TILE = 128
BLOCK = 512
COARSE = 2048
K_CAND = 8
D = 768
NY, NX, NZ = 4, 4, 4
TILES = NX * NZ
BIG = 1 << 20
F32 = jnp.float32
BF16 = jnp.bfloat16
MESH = pl.DeviceIdType.MESH
THIRD = D // 3
HALF = D // 2
NEAR = 64
REST = TILE - NEAR


def mm(a, b, ca, cb):
    return lax.dot_general(a, b, (((ca,), (cb,)), ((), ())), preferred_element_type=F32)


def delta_of(scores, labels, positives):
    hit = labels == positives[0:1]
    for p in range(1, 4):
        hit = hit | (labels == positives[p : p + 1])
    return (0.125 * jnp.tanh(0.5 * scores) + jnp.where(hit, -0.125, 0.125)).astype(BF16)


class Place:
    def __init__(self):
        grp, mid = lax.axis_index("grp"), lax.axis_index("mid")
        self.y, self.c = grp // 2, lax.rem(grp, 2)
        self.x, self.z = mid // NZ, lax.rem(mid, NZ)
        self.mid = mid
        self.ahead = 1 + 2 * self.c
        self.behind = 3 - 2 * self.c

    def at(self, dy=0, dx=0, dz=0, other=False):
        y, x, z = lax.rem(self.y + dy, NY), lax.rem(self.x + dx, NX), lax.rem(self.z + dz, NZ)
        return (2 * y + (1 - self.c if other else self.c), NZ * x + z)

    def sibling(self):
        return (2 * self.y + 1 - self.c, self.mid)

    def tile(self, dx, dz):
        return NZ * lax.rem(self.x + dx, NX) + lax.rem(self.z + dz, NZ)

    def greet(self):
        near = [self.sibling(), self.at(dy=2)]
        for step in (self.ahead, self.behind):
            near += [self.at(dy=step), self.at(dy=step, other=True)]
            near += [self.at(dx=step), self.at(dz=step)]
        barrier = pltpu.get_barrier_semaphore()
        for device in near:
            pl.semaphore_signal(barrier, inc=1, device_id=device, device_id_type=MESH)
        pl.semaphore_wait(barrier, len(near))


class Net:
    def __init__(self, send_sem, recv_sem):
        self.send_sem, self.recv_sem, self.made = send_sem, recv_sem, []

    def send(self, src, dst, device):
        i = len(self.made)
        copy = pltpu.make_async_remote_copy(
            src_ref=src,
            dst_ref=dst,
            send_sem=self.send_sem.at[i],
            recv_sem=self.recv_sem.at[i],
            device_id=device,
            device_id_type=MESH,
        )
        copy.start()
        self.made.append(copy)
        return copy

    def finish(self):
        for copy in self.made:
            copy.wait_send()


COPIES = 200
OWN, BACK, FRONT, ACROSS = range(4)
SLOTS = 32
LIST = 16


def role_step(color, role):
    return (0, 3 - 2 * color, 1 + 2 * color, 2)[role]


def main_kernel(
    q, mp, lp, mc, lc, cp, owner, cv, midv, leafv,
    gq, gco, plan, sel, deltas,
    q_own, q_b, q_a, q_2, p_own, cvv, cvm, cpall,
    in00, in01, in02, in03, in10, in11, in12, in13,
    no00, no01, no02, no03, no10, no11, no12, no13,
    sm00, sm01, sm02, sm03, sm10, sm11, sm12, sm13,
    no_a, no_b, no_x, planv, smo, pk_as, pk_ao, pk_bs, pk_bo, pk_own, pk_x, pk_b, pk_f,
    out_own, out_x, out0b, out0f, out1o, out1b, out1f, out1x,
    ret_own, ret_x, a0_0, a0_1, a1_0, a1_1, b0_0, b0_1, b1_0, b1_1,
    vectors, held_delta, gc, qc, gsib, gbuf,
    s2, sb, r2, rb, ra, u2, ub, ua, far, local_sem, send_sem, recv_sem,
):
    me = Place()
    c, a, b = me.c, me.ahead, me.behind
    net = Net(send_sem, recv_sem)
    local, done = [], []

    def start_local(src, dst):
        copy = pltpu.make_async_copy(src, dst, local_sem.at[len(local)])
        copy.start()
        local.append(copy)
        return copy

    def wait_local(copy):
        copy.wait()
        done.append(copy)

    load_q = start_local(q, q_own)
    load_v = [start_local(midv, vectors.at[pl.ds(0, 4)]), start_local(leafv, vectors.at[pl.ds(4, 2)])]
    load_c = start_local(cv, cvv)
    for t in range(TILES):
        p_own[t, 0:4, :] = mp[:, t * TILE : (t + 1) * TILE]
        p_own[t, 4:8, :] = lp[:, t * TILE : (t + 1) * TILE]
    p_own[16:18] = jnp.full((2, 8, 128), -1, jnp.int32)
    p_own[16, :, 0:TILES] = mc[...]
    p_own[17, :, 0:TILES] = lc[...]
    cpall[me.x, me.z, 0:4, :] = cp[...]
    cpall[me.x, me.z, 4:8, :] = cp[...]
    me.greet()

    m = me.mid
    up, down, across = me.at(dy=a), me.at(dy=b), me.at(dy=2)
    up_other, down_other = me.at(dy=a, other=True), me.at(dy=b, other=True)
    xa, xb, za, zb = me.at(dx=a), me.at(dx=b), me.at(dz=a), me.at(dz=b)
    sib = me.sibling()
    planes = {BACK: q_b, FRONT: q_a, ACROSS: q_2}
    slots = ((in00, in01, in02, in03), (in10, in11, in12, in13))
    notes = ((no00, no01, no02, no03), (no10, no11, no12, no13))
    facts = ((sm00, sm01, sm02, sm03), (sm10, sm11, sm12, sm13))
    outs = ((out_own, out0b, out0f, out_x), (out1o, out1b, out1f, out1x))

    rest, near = pl.ds(NEAR, REST), pl.ds(0, NEAR)
    y_in = {
        BACK: net.send(q.at[m, rest], q_b.at[m], up),
        FRONT: net.send(q.at[m, rest], q_a.at[m], down),
        ACROSS: net.send(q.at[m], q_2.at[m], across),
    }
    pos_own = cpall.at[me.x, me.z]
    cz_a = net.send(pos_own, pos_own, za)
    cz_b = net.send(pos_own, pos_own, zb)

    index = lax.broadcasted_iota(jnp.int32, (2, 128), 0) * 128 + lax.broadcasted_iota(
        jnp.int32, (2, 128), 1
    )
    code = 4 * (
        TILES * lax.broadcasted_iota(jnp.int32, (8, 128), 0)
        + lax.broadcasted_iota(jnp.int32, (8, 128), 1)
    )
    lane = lax.broadcasted_iota(jnp.int32, (1, 128), 1)
    mids, leaves = p_own[16], p_own[17]
    for label, step in enumerate((0, a, b, 2)):
        for which, core in enumerate((c, 1 - c)):
            device = (2 * lax.rem(me.y + step, NY) + core) * TILES + m
            held = [
                jnp.sum(
                    jnp.where(owner[...] == 2 * device + i, index, 0), axis=(0, 1), keepdims=True
                )
                for i in range(2)
            ]
            entries = []
            for live, block in (
                ((mids >> 2) == device, mids & 3),
                ((leaves == held[0]) | (leaves == held[1]), (leaves == held[1]).astype(jnp.int32)),
            ):
                found = code + block
                first = jnp.min(jnp.where(live, found, BIG), axis=(0, 1), keepdims=True)
                final = jnp.max(jnp.where(live, found, -1), axis=(0, 1), keepdims=True)
                some = first < BIG
                entries.append((some, jnp.where(some, first, 0)))
                two = some & (final != first)
                entries.append((two, jnp.where(two, final, 0)))
            tiles = [(value >> 2) & 15 for _, value in entries]
            spots = jnp.full((1, 128), 4, jnp.int32)
            for e in (3, 2, 1, 0):
                spots = jnp.where(entries[e][0] & (tiles[e] == lane), e, spots)
            at = 32 + 2 * label + which
            planv[at : at + 1, :] = spots
            for e, (valid, value) in enumerate(entries):
                slot = jnp.full((1, 1), e, jnp.int32)
                for f in range(e - 1, -1, -1):
                    slot = jnp.where(valid & entries[f][0] & (tiles[f] == tiles[e]), f, slot)
                row = jnp.where(lane == 0, jnp.where(valid, value & 3, -1), slot)
                row = jnp.where(lane == 2, tiles[e], row)
                row = jnp.where(lane == 3, value >> 6, row)
                row = jnp.where(lane == 4, (value & 3) + 4 * (e // 2), row)
                at = 8 * label + 4 * which + e
                planv[at : at + 1, :] = row
    to_smem = start_local(planv, smo)
    wait_local(load_q)
    wait_local(to_smem)
    notes_out = (no00, no_a, no_b, no_x)

    def fill_notes(label):
        out = notes_out[label]
        for e in range(8):
            at = 8 * label + e
            level = 4 * (e % 4 // 2)
            positives = p_own[smo[at, 2]][level : level + 4] - BLOCK * smo[at, 3]
            out[e, 0:4, :] = positives
            out[e, 4:5, :] = planv[at : at + 1, :]
            out[e, 5:8, :] = jnp.zeros((3, 128), jnp.int32)
        out[8, 0:2, :] = planv[32 + 2 * label : 34 + 2 * label, :]
        out[8, 2:8, :] = jnp.zeros((6, 128), jnp.int32)

    direct, note_in = {}, {}
    for label, targets in ((BACK, ((pk_as, up), (pk_ao, up_other))), (FRONT, ((pk_bs, down), (pk_bo, down_other)))):
        fill_notes(label)
        for which, (buffer, device) in enumerate(targets):
            for e in range(4):
                buffer[e] = q_own[smo[8 * label + 4 * which + e, 2], 0:NEAR]
            note_in[which, label] = net.send(notes_out[label], notes[which][label], device)
            direct[which, label] = net.send(buffer, slots[which][label].at[:, near], device)
    fill_notes(ACROSS)
    note_in[0, ACROSS] = net.send(no_x, no03, across)
    fill_notes(OWN)
    for e in range(4):
        pk_own[e] = q_own[smo[4 + e, 2]]
    note_in[1, OWN] = net.send(no00, no10, sib)
    beside = {OWN: net.send(pk_own, in10, sib)}
    for e in range(4):
        in00[e] = q_own[smo[e, 2]]

    axes = ((za, zb, xa, xb), (xa, xb, za, zb))
    walk = (0, b, a, 2)

    def rows_of(role, h):
        size = (TILE if role == ACROSS else REST) // 2
        return pl.ds(h * size, size)

    def tile_of(h, first, last):
        return me.tile(last, first) if h == 0 else me.tile(first, last)

    second, second_f, last, last_f = {}, {}, {}, {}

    def send_second(role):
        y_in[role].wait_recv()
        for h, (to_a, to_b, _, _) in enumerate(axes):
            piece = planes[role].at[m, rows_of(role, h)]
            second[role, h] = (net.send(piece, piece, to_a), net.send(piece, piece, to_b))

    def send_last(role, key):
        for h, (_, _, to_a, to_b) in enumerate(axes):
            piece = planes[role].at[tile_of(h, walk[key], 0), rows_of(role, h)]
            last[role, h, key] = (net.send(piece, piece, to_a), net.send(piece, piece, to_b))

    def second_stage(role):
        for h, (to_a, _, _, _) in enumerate(axes):
            second[role, h][0].wait_recv()
            piece = planes[role].at[tile_of(h, b, 0), rows_of(role, h)]
            second_f[role, h] = net.send(piece, piece, to_a)
        send_last(role, BACK)
        for h in range(2):
            second[role, h][1].wait_recv()
        send_last(role, FRONT)

    def across_stage(role):
        for h in range(2):
            second_f[role, h].wait_recv()
        send_last(role, ACROSS)

    def forward_last(role):
        for key, step in enumerate(walk):
            for h, (_, _, to_a, _) in enumerate(axes):
                last[role, h, key][0].wait_recv()
                piece = planes[role].at[tile_of(h, step, b), rows_of(role, h)]
                last_f[role, h, key] = net.send(piece, piece, to_a)

    def complete(role):
        for key in range(4):
            for h in range(2):
                last[role, h, key][1].wait_recv()
                last_f[role, h, key].wait_recv()

    def know(which, role):
        if (which, role) in note_in:
            note_in[which, role].wait_recv()
        wait_local(start_local(notes[which][role], facts[which][role]))

    def pack(role):
        know(0, role)
        rows = planes[role]
        buffer = {BACK: pk_b, FRONT: pk_f, ACROSS: pk_x}[role]
        for e in range(4):
            buffer[e] = rows[facts[0][role][4 + e, 4, 2]]
        if role == ACROSS:
            note_in[1, role] = net.send(no03, no13, sib)
            beside[role] = net.send(buffer, in13, sib)
        else:
            beside[role] = net.send(buffer, slots[1][role].at[:, rest], sib)
        for e in range(4):
            value = rows[facts[0][role][e, 4, 2]]
            if role == ACROSS:
                in03[e] = value
            else:
                slots[0][role][e, NEAR:TILE] = value

    labels = lax.broadcasted_iota(jnp.int32, (BLOCK, TILE), 0)
    returns = {}

    def pairs(which, role):
        if which == 1:
            know(1, role)
            beside[role].wait_recv()
        if (which, role) in direct:
            direct[which, role].wait_recv()
        block_of, rows, info, out = (
            facts[which][role], slots[which][role], notes[which][role], outs[which][role]
        )
        group = pl.ds(4 * role, 4)
        start_local(rows, sel.at[which, group])

        def body(e, carry):
            block = vectors[block_of[4 * which + e, 4, 4]]
            delta = delta_of(mm(block, rows[e], 1, 1), labels, info[4 * which + e])
            held_delta[which, 4 * role + e] = delta
            out[e] = mm(delta, block, 0, 0).astype(BF16)
            return carry

        lax.fori_loop(0, 4, body, 0)
        start_local(held_delta.at[which, group], deltas.at[which, group])
        for e in range(3):
            value = out[e]
            for f in range(e + 1, 4):
                same = block_of[4 * which + f, 4, 1] == e
                value += jnp.where(same, out[f], jnp.zeros((TILE, D), BF16))
            out[e] = value
        for e in range(4):
            at = 16 * which + 4 * role + e
            plan[at : at + 1, :] = info[4 * which + e, 4:5, :]

    row_halves = (pl.ds(0, TILE // 2), pl.ds(TILE // 2, TILE // 2))
    ret_a0, ret_a1, ret_b0, ret_b1 = (a0_0, a0_1), (a1_0, a1_1), (b0_0, b0_1), (b1_0, b1_1)
    four = pl.ds(0, 4)

    def give_back(which, role, r):
        out = outs[which][role]
        back = {
            (0, BACK): (ret_a0, down),
            (0, FRONT): (ret_b0, up),
            (1, BACK): (ret_a1, up_other),
            (1, FRONT): (ret_b1, down_other),
        }[which, role]
        returns[which, role, r] = net.send(
            out.at[four, row_halves[r]], back[0][r].at[four], back[1]
        )

    for ref in (out_own, out_x, ret_own, ret_x):
        ref[4] = jnp.zeros((TILE, D), BF16)
    for ref in ret_a0 + ret_a1 + ret_b0 + ret_b1:
        ref[4] = jnp.zeros((TILE // 2, D), BF16)
    steps = (0, b, a, 2)
    first_axis = ((xa, xb), (za, zb))
    first2, firsta, firstb = {}, {}, {}
    second2, seconda, secondb = {}, {}, {}
    term_in = {}

    def part(h, stream, unit, j):
        tile = me.tile(steps[unit], steps[j]) if h == 0 else me.tile(steps[j], steps[unit])
        cols = slice(h * HALF, (h + 1) * HALF)
        r = stream % 2
        rows = slice(r * TILE // 2, (r + 1) * TILE // 2)
        if stream < 2:
            return out_x[sm03[8, 0, tile], rows, cols] + ret_x[sm03[8, 1, tile], rows, cols]
        value = out_own[smo[32 + 2 * OWN, tile], rows, cols]
        value += ret_own[smo[33 + 2 * OWN, tile], rows, cols]
        value += ret_a0[r][smo[32 + 2 * BACK, tile], :, cols]
        value += ret_a1[r][smo[33 + 2 * BACK, tile], :, cols]
        value += ret_b0[r][smo[32 + 2 * FRONT, tile], :, cols]
        return value + ret_b1[r][smo[33 + 2 * FRONT, tile], :, cols]

    def begin_sum(stream):
        if stream == 0:
            term_in[ACROSS].wait_recv()
        if stream >= 2:
            if stream == 2:
                term_in[OWN].wait_recv()
            for which in range(2):
                for role in (BACK, FRONT):
                    returns[which, role, stream - 2].wait_recv()
        for h in range(2):
            for j in range(4):
                s2[h, stream, j] = part(h, stream, ACROSS, j)
            first2[h, stream] = net.send(s2.at[h, stream], r2.at[h, stream], first_axis[h][0])
            for j in range(4):
                sb[h, stream, j] = part(h, stream, BACK, j)
            firstb[h, stream] = net.send(sb.at[h, stream], rb.at[h, stream], first_axis[h][1])

    def pass_sum(stream):
        for h in range(2):
            first2[h, stream].wait_recv()
            for j in range(4):
                r2[h, stream, j] = r2[h, stream, j] + part(h, stream, FRONT, j)
            firsta[h, stream] = net.send(r2.at[h, stream], ra.at[h, stream], first_axis[h][0])

    def begin_second(stream):
        for h in range(2):
            firstb[h, stream].wait_recv()
            firsta[h, stream].wait_recv()
            to_a, to_b = first_axis[1 - h]
            for j in (ACROSS, BACK, FRONT, OWN):
                rb[h, stream, j] = part(h, stream, OWN, j) + rb[h, stream, j] + ra[h, stream, j]
                if j == ACROSS:
                    second2[h, stream] = net.send(rb.at[h, stream, j], u2.at[h, stream], to_a)
                if j == BACK:
                    secondb[h, stream] = net.send(rb.at[h, stream, j], ub.at[h, stream], to_b)

    def pass_second(stream):
        for h in range(2):
            second2[h, stream].wait_recv()
            u2[h, stream] = u2[h, stream] + rb[h, stream, FRONT]
            seconda[h, stream] = net.send(u2.at[h, stream], ua.at[h, stream], first_axis[1 - h][0])

    def end_second(stream):
        for h in range(2):
            secondb[h, stream].wait_recv()
            seconda[h, stream].wait_recv()
            ub[h, stream] = rb[h, stream, OWN] + ub[h, stream] + ua[h, stream]

    send_second(BACK)
    send_second(FRONT)
    send_last(BACK, OWN)
    send_second(ACROSS)
    know(0, OWN)
    for load in load_v:
        wait_local(load)
    pairs(0, OWN)
    second_stage(BACK)
    cz_a.wait_recv()
    pos_b = cpall.at[me.x, lax.rem(me.z + b, NZ)]
    cz_f = net.send(pos_b, pos_b, za)
    send_last(FRONT, OWN)
    second_stage(FRONT)
    across_stage(BACK)
    pairs(1, OWN)
    term_in[OWN] = net.send(out1o, ret_own.at[four], sib)
    across_stage(FRONT)
    cz_b.wait_recv()
    cz_f.wait_recv()
    pos_row = cpall.at[me.x]
    cx_a = net.send(pos_row, pos_row, xa)
    cx_b = net.send(pos_row, pos_row, xb)
    forward_last(BACK)
    send_last(ACROSS, OWN)
    second_stage(ACROSS)
    complete(BACK)
    pack(BACK)
    across_stage(ACROSS)
    cx_a.wait_recv()
    pos_row_b = cpall.at[lax.rem(me.x + b, NX)]
    cx_f = net.send(pos_row_b, pos_row_b, xa)
    pairs(0, BACK)
    give_back(0, BACK, 0)
    forward_last(FRONT)
    complete(FRONT)
    pack(FRONT)
    pairs(0, FRONT)
    give_back(0, FRONT, 0)
    forward_last(ACROSS)
    pairs(1, BACK)
    give_back(1, BACK, 0)
    pairs(1, FRONT)
    give_back(1, FRONT, 0)
    for role in (BACK, FRONT):
        for which in range(2):
            give_back(which, role, 1)
    wait_local(load_c)
    for j in range(8):
        color, role = j // 4, j % 4
        row = (2 * lax.rem(me.y + role_step(color, role), NY) + color) * TILES + m
        start = pl.multiple_of(row * 16, 16)
        cvm[pl.ds(16 * j, 16), :] = cvv[pl.ds(start, 16), :]
    place = lax.broadcasted_iota(jnp.int32, (128, 128), 0)
    chunk = place // 16
    color, role = chunk // 4, lax.rem(chunk, 4)
    step = jnp.where(role == ACROSS, 2, jnp.where(role == FRONT, 1 + 2 * color, 3 - 2 * color))
    step = jnp.where(role == OWN, 0, step)
    owner_grp = 2 * lax.rem(me.y + step, NY) + color
    coarse_ids = (owner_grp * TILES + m) * 16 + lax.rem(place, 16)

    def own_coarse():
        qm = q_own[m]
        total = jnp.zeros((TILE, D), F32)
        for i in range(COARSE // BLOCK):
            vectors = cvv[i * BLOCK : (i + 1) * BLOCK, :]
            labels = lax.broadcasted_iota(jnp.int32, (BLOCK, TILE), 0) + i * BLOCK
            delta = delta_of(mm(vectors, qm, 1, 1), labels, cpall[me.x, me.z])
            total += mm(delta, vectors, 0, 0)
        qc[...] = total

    def rows_coarse(lo, hi):
        def body(t, carry):
            qt = q_own[t]
            delta = delta_of(mm(cvm[...], qt, 1, 1), coarse_ids, cpall[t // NZ, lax.rem(t, NZ)])
            gc[...] += mm(delta, qt, 1, 0)
            return carry

        lax.fori_loop(lo, hi, body, 0)


    gc[...] = jnp.zeros_like(gc)
    own_coarse()
    complete(ACROSS)
    pack(ACROSS)
    cx_b.wait_recv()
    cx_f.wait_recv()
    pairs(0, ACROSS)
    rows_coarse(0, 8)
    pairs(1, ACROSS)
    term_in[ACROSS] = net.send(out1x, ret_x.at[four], sib)
    rows_coarse(8, 16)
    coarse = net.send(gc.at[pl.ds(64 * (1 - c), 64)], gsib, sib)
    begin_sum(2)
    begin_sum(0)
    begin_sum(1)
    pass_sum(2)
    pass_sum(0)
    pass_sum(1)
    begin_sum(3)
    begin_second(2)
    begin_second(0)
    begin_second(1)
    pass_sum(3)
    pass_second(2)
    pass_second(0)
    pass_second(1)
    coarse.wait_recv()
    for role in range(4):
        gbuf[role] = gc[pl.ds(64 * c + 16 * role, 16)] + gsib[16 * role : 16 * role + 16]
    coarse2 = net.send(gbuf.at[ACROSS], gbuf.at[5], up)
    coarseb = net.send(gbuf.at[BACK], gbuf.at[6], down)
    end_second(0)
    end_second(1)
    home = net.send(ub.at[:, pl.ds(0, 2)], far, across)
    begin_second(3)
    end_second(2)
    coarse2.wait_recv()
    gbuf[4] = gbuf[FRONT] + gbuf[5]
    coarsea = net.send(gbuf.at[4], gbuf.at[7], up)
    pass_second(3)
    coarsea.wait_recv()
    coarseb.wait_recv()
    gco[...] = gbuf[OWN] + gbuf[6] + gbuf[7]
    home.wait_recv()
    end_second(3)
    for h in range(2):
        cols = slice(h * HALF, (h + 1) * HALF)
        for r in range(2):
            rows = slice(r * TILE // 2, (r + 1) * TILE // 2)
            gq[rows, cols] = (
                qc[rows, cols] + ub[h, 2 + r].astype(F32) + far[h, r].astype(F32)
            )
    for copy in local:
        if not any(copy is other for other in done):
            copy.wait()
    net.finish()


def grads_kernel(
    plan, sel, deltas,
    gm, gl,
    counts, entries, rows, held, acc, row_sem, delta_sem, grad_sem,
):
    stores = [(gm, 0), (gm, 1), (gm, 2), (gm, 3), (gl, 0), (gl, 1)]

    def row_copy(e):
        return pltpu.make_async_copy(sel.at[e], rows.at[e], row_sem.at[e])

    def delta_copy(e):
        return pltpu.make_async_copy(deltas.at[e], held.at[e], delta_sem.at[e])

    for key in range(6):
        counts[key] = 0
    for e in range(SLOTS):
        block = plan[e, 0]

        @pl.when(block >= 0)
        def _():
            row_copy(e).start()
            delta_copy(e).start()
            key = block + 4 * (e // 2 % 2)
            n = counts[key]
            entries[LIST * key + n] = e
            counts[key] = n + 1

    rows[SLOTS] = jnp.zeros((TILE, D), BF16)
    held[SLOTS] = jnp.zeros((BLOCK, TILE), BF16)

    def per_key(key, carry):
        n = counts[key]
        start = LIST * key

        @pl.when(n == 0)
        def _():
            acc[key] = jnp.zeros((BLOCK, D), F32)

        def batch(i, inner):
            at = start + 2 * i
            full = 2 * i + 1 < n
            e0 = entries[at]
            e1 = jnp.where(full, entries[at + 1], SLOTS)
            row_copy(e0).wait()
            delta_copy(e0).wait()

            @pl.when(full)
            def _():
                row_copy(e1).wait()
                delta_copy(e1).wait()

            both = jnp.concatenate([rows[e0], rows[e1]], axis=0)
            delta = jnp.concatenate([held[e0], held[e1]], axis=1)

            @pl.when(i == 0)
            def _():
                for n_col in range(3):
                    cols = slice(n_col * THIRD, (n_col + 1) * THIRD)
                    acc[key, :, cols] = mm(delta, both[:, cols], 1, 0)

            @pl.when(i != 0)
            def _():
                for n_col in range(3):
                    cols = slice(n_col * THIRD, (n_col + 1) * THIRD)
                    acc[key, :, cols] += mm(delta, both[:, cols], 1, 0)

            return inner

        lax.fori_loop(0, (n + 1) // 2, batch, 0)
        for i, (out, j) in enumerate(stores):

            @pl.when(key == i)
            def _():
                pltpu.make_async_copy(acc.at[i], out.at[j], grad_sem.at[i]).start()

        return carry

    lax.fori_loop(0, 6, per_key, 0)
    for i, (out, j) in enumerate(stores):
        pltpu.make_async_copy(acc.at[i], out.at[j], grad_sem.at[i]).wait()


def vmem():
    return pl.BlockSpec(memory_space=pltpu.VMEM)


def smem():
    return pl.BlockSpec(memory_space=pltpu.SMEM)


def hbm():
    return pl.BlockSpec(memory_space=pl.ANY)


def shape(dims, dtype):
    return jax.ShapeDtypeStruct(dims, dtype)


def shards(
    queries,
    coarse_vectors,
    mid_vectors,
    leaf_vectors,
    coarse_pos,
    mid_pos,
    leaf_pos,
    mid_cand,
    leaf_cand,
    leaf_owner,
):
    dma = pltpu.SemaphoreType.DMA
    mib = 1024 * 1024
    group = pltpu.VMEM((TILES, TILE, D), BF16)
    part = pltpu.VMEM((TILES, REST, D), BF16)
    four = pltpu.VMEM((4, TILE, D), BF16)
    five = pltpu.VMEM((5, TILE, D), BF16)
    half = pltpu.VMEM((5, TILE // 2, D), BF16)
    near = pltpu.VMEM((4, NEAR, D), BF16)
    rest = pltpu.VMEM((4, REST, D), BF16)
    notes = pltpu.VMEM((9, 8, 128), jnp.int32)
    facts = pltpu.SMEM((9, 8, 128), jnp.int32)
    first = pltpu.VMEM((2, 4, 4, TILE // 2, HALF), BF16)
    second = pltpu.VMEM((2, 4, TILE // 2, HALF), BF16)
    gq, gco, plan, sel, deltas = pl.pallas_call(
        main_kernel,
        out_shape=(
            shape((TILE, D), F32),
            shape((16, D), F32),
            shape((SLOTS, 128), jnp.int32),
            shape((2, 16, TILE, D), BF16),
            shape((2, 16, BLOCK, TILE), BF16),
        ),
        in_specs=[hbm(), vmem(), vmem(), vmem(), vmem(), vmem(), vmem(), hbm(), hbm(), hbm()],
        out_specs=(vmem(), vmem(), vmem(), hbm(), hbm()),
        scratch_shapes=[
            group, part, part, group,
            pltpu.VMEM((18, 8, 128), jnp.int32),
            pltpu.VMEM((COARSE, D), BF16),
            pltpu.VMEM((128, D), BF16),
            pltpu.VMEM((NX, NZ, 8, TILE), jnp.int32),
            four, four, four, four, four, four, four, four,
            notes, notes, notes, notes, notes, notes, notes, notes,
            facts, facts, facts, facts, facts, facts, facts, facts,
            notes, notes, notes,
            pltpu.VMEM((40, 128), jnp.int32),
            pltpu.SMEM((40, 128), jnp.int32),
            near, near, near, near, four, four, rest, rest,
            five, five, four, four, four, four, four, four,
            five, five,
            half, half, half, half, half, half, half, half,
            pltpu.VMEM((6, BLOCK, D), BF16),
            pltpu.VMEM((2, 16, BLOCK, TILE), BF16),
            pltpu.VMEM((128, D), F32),
            pltpu.VMEM((TILE, D), F32),
            pltpu.VMEM((64, D), F32),
            pltpu.VMEM((8, 16, D), F32),
            first, first, first, first, first,
            second, second, second,
            pltpu.VMEM((2, 2, TILE // 2, HALF), BF16),
            dma((40,)),
            dma((COPIES,)),
            dma((COPIES,)),
        ],
        compiler_params=pltpu.CompilerParams(
            collective_id=0, has_side_effects=True, vmem_limit_bytes=62 * mib
        ),
        name="main",
    )(
        queries.reshape(TILES, TILE, D),
        mid_pos.T,
        leaf_pos.T,
        mid_cand.T,
        leaf_cand.T,
        coarse_pos.T,
        leaf_owner.reshape(2, 128),
        coarse_vectors,
        mid_vectors.reshape(4, BLOCK, D),
        leaf_vectors.reshape(2, BLOCK, D),
    )
    gm, gl = pl.pallas_call(
        grads_kernel,
        out_shape=(shape((4, BLOCK, D), F32), shape((2, BLOCK, D), F32)),
        in_specs=[smem(), hbm(), hbm()],
        out_specs=(hbm(), hbm()),
        scratch_shapes=[
            pltpu.SMEM((6,), jnp.int32),
            pltpu.SMEM((6 * LIST + 1,), jnp.int32),
            pltpu.VMEM((SLOTS + 1, TILE, D), BF16),
            pltpu.VMEM((SLOTS + 1, BLOCK, TILE), BF16),
            pltpu.VMEM((6, BLOCK, D), F32),
            dma((SLOTS,)),
            dma((SLOTS,)),
            dma((6,)),
        ],
        compiler_params=pltpu.CompilerParams(vmem_limit_bytes=60 * mib),
        name="grads",
    )(plan, sel.reshape(SLOTS, TILE, D), deltas.reshape(SLOTS, BLOCK, TILE))
    return gq, gco, gm.reshape(4 * BLOCK, D), gl.reshape(2 * BLOCK, D)


def solution(mesh):
    placed = (
        P("grp", None),
        P(),
        P(("grp", "mid"), None),
        P(("grp", "mid"), None),
        P(("grp", "mid"), None),
        P("grp", None),
        P("grp", None),
        P("grp", None),
        P("grp", None),
        P(),
    )
    return jax.shard_map(
        shards,
        mesh=mesh,
        in_specs=placed,
        out_specs=(
            P(("grp", "mid"), None),
            P(("grp", "mid"), None),
            P(("grp", "mid"), None),
            P(("grp", "mid"), None),
        ),
        check_vma=False,
    )
```

time: 166 us -> 135 us (0.81); the launches traced: 164 us -> 134 us
  Pallas kernels: 156 us -> 132 us
  local copies, waits for them, and re-layouts: 7.06 us -> 1.38 us
    pallas_call x1, Pallas kernels: 141 us -> 123 us  [shards(): pl.pallas_call(main_kernel, out_shape=(shape((TILE, D), F32), shape((16,...]
    unnamed x12 -> x6, local copies, waits for them, and re-layouts: 7.06 us -> 1.38 us
    pallas_call x1, Pallas kernels: 14.8 us -> 9.1 us  [shards(): pl.pallas_call(grads_kernel, out_shape=(shape((4, BLOCK, D), F32), shape(...]
where the time goes in v3:
time: 135 us; the launch traced here: 134 us
  Pallas kernels  132 us (98%)
  local copies, waits for them, and re-layouts  1.38 us (1%)
    pallas_call x1, Pallas kernels, shards(): pl.pallas_call(main_kernel, out_shape=(shape((TILE, D), F32), shape((16,...  123 us
    pallas_call x1, Pallas kernels, shards(): pl.pallas_call(grads_kernel, out_shape=(shape((4, BLOCK, D), F32), shape(...  9.1 us

profile of v3, /device:TPU:0, one launch (start us, length us, event | category | flops | bytes accessed | tf_op | source)
XLA Modules:
  0.0 134.4 jit_solution(2212518137109440542)
XLA Ops:
  0.6 123.3 %main.1 = (f32[128,768]{1,0:T(8,128)}, f32[16,768]{1,0:T(8,128)}, s32[32,128]{1,0:T(8,128)}, bf16[2,16,128,768]{3,2,1,0:T(8,128)(2,1)}, bf16[2,16,512,128]{3,2,1,0:T(8,128)(2,1)}) custom-call(bf16[16,128,768]{2,1,0:T(8,128)(2,1)} %bitcast.15, s32[4,2048]{1,0:T(4,128)} %bitcast.18, s32[4,2048]{1,0:T(4,128)} %bitcast.19, s32[8,16]{1,0:T(8,128)} %bitcast.20, ...), custom_call_target="tpu_custom_call" | custom-call | tf_op jit(solution)/shard_map/main/pallas_call | solution.py:700
  123.9 0.0 copy-start
  123.9 0.0 copy-start.1
  123.9 9.1 %grads.1 = (f32[4,512,768]{2,1,0:T(8,128)}, f32[2,512,768]{2,1,0:T(8,128)}) custom-call(s32[32,128]{1,0:T(8,128)} %get-tuple-element.13.plan, bf16[32,128,768]{2,1,0:T(8,128)(2,1)} %bitcast.13, bf16[32,512,128]{2,1,0:T(8,128)(2,1)} %bitcast.14), custom_call_target="tpu_custom_call" | custom-call | tf_op jit(solution)/shard_map/grads/pallas_call | solution.py:756
  133.0 0.0 copy-done
  133.0 0.7 copy.16
  133.8 0.0 copy-done.1
  133.8 0.6 copy.17
Async XLA Ops:
  123.9 9.1 %copy-start = (f32[128,768]{1,0:T(8,128)S(1)}, f32[128,768]{1,0:T(8,128)}, u32[]{:S(2)}) copy-start(f32[128,768]{1,0:T(8,128)} %get-tuple-element.22) | copy-start | bytes 1179652
  123.9 9.9 %copy-start.1 = (f32[16,768]{1,0:T(8,128)S(1)}, f32[16,768]{1,0:T(8,128)}, u32[]{:S(2)}) copy-start(f32[16,768]{1,0:T(8,128)} %get-tuple-element.23) | copy-start | bytes 147460

commit v4 on v3

--- a/solution.py
+++ b/solution.py
@@ -167,12 +167,18 @@
     )
     lane = lax.broadcasted_iota(jnp.int32, (1, 128), 1)
     mids, leaves = p_own[16], p_own[17]
+
+    def whole(value):
+        return jnp.broadcast_to(value, (1, 128))
+
     for label, step in enumerate((0, a, b, 2)):
         for which, core in enumerate((c, 1 - c)):
             device = (2 * lax.rem(me.y + step, NY) + core) * TILES + m
             held = [
-                jnp.sum(
-                    jnp.where(owner[...] == 2 * device + i, index, 0), axis=(0, 1), keepdims=True
+                whole(
+                    jnp.sum(
+                        jnp.where(owner[...] == 2 * device + i, index, 0), axis=(0, 1), keepdims=True
+                    )
                 )
                 for i in range(2)
             ]
@@ -182,8 +188,8 @@
                 ((leaves == held[0]) | (leaves == held[1]), (leaves == held[1]).astype(jnp.int32)),
             ):
                 found = code + block
-                first = jnp.min(jnp.where(live, found, BIG), axis=(0, 1), keepdims=True)
-                final = jnp.max(jnp.where(live, found, -1), axis=(0, 1), keepdims=True)
+                first = whole(jnp.min(jnp.where(live, found, BIG), axis=(0, 1), keepdims=True))
+                final = whole(jnp.max(jnp.where(live, found, -1), axis=(0, 1), keepdims=True))
                 some = first < BIG
                 entries.append((some, jnp.where(some, first, 0)))
                 two = some & (final != first)
@@ -195,10 +201,10 @@
             at = 32 + 2 * label + which
             planv[at : at + 1, :] = spots
             for e, (valid, value) in enumerate(entries):
-                slot = jnp.full((1, 1), e, jnp.int32)
-                for f in range(e - 1, -1, -1):
-                    slot = jnp.where(valid & entries[f][0] & (tiles[f] == tiles[e]), f, slot)
-                row = jnp.where(lane == 0, jnp.where(valid, value & 3, -1), slot)
+                follow = jnp.full((1, 128), 4, jnp.int32)
+                for f in range(3, e, -1):
+                    follow = jnp.where(valid & entries[f][0] & (tiles[f] == tiles[e]), f, follow)
+                row = jnp.where(lane == 0, jnp.where(valid, value & 3, -1), follow)
                 row = jnp.where(lane == 2, tiles[e], row)
                 row = jnp.where(lane == 3, value >> 6, row)
                 row = jnp.where(lane == 4, (value & 3) + 4 * (e // 2), row)
@@ -290,10 +296,15 @@
                 last[role, h, key][1].wait_recv()
                 last_f[role, h, key].wait_recv()
 
-    def know(which, role):
+    fetches = {}
+
+    def fetch(which, role):
         if (which, role) in note_in:
             note_in[which, role].wait_recv()
-        wait_local(start_local(notes[which][role], facts[which][role]))
+        fetches[which, role] = start_local(notes[which][role], facts[which][role])
+
+    def know(which, role):
+        wait_local(fetches[which, role])
 
     def pack(role):
         know(0, role)
@@ -301,10 +312,10 @@
         buffer = {BACK: pk_b, FRONT: pk_f, ACROSS: pk_x}[role]
         for e in range(4):
             buffer[e] = rows[facts[0][role][4 + e, 4, 2]]
-        if role == ACROSS:
-            note_in[1, role] = net.send(no03, no13, sib)
-            beside[role] = net.send(buffer, in13, sib)
-        else:
+            if role == ACROSS and e % 2:
+                duo = pl.ds(e - 1, 2)
+                beside[role, e // 2] = net.send(buffer.at[duo], in13.at[duo], sib)
+        if role != ACROSS:
             beside[role] = net.send(buffer, slots[1][role].at[:, rest], sib)
         for e in range(4):
             value = rows[facts[0][role][e, 4, 2]]
@@ -316,36 +327,34 @@
     labels = lax.broadcasted_iota(jnp.int32, (BLOCK, TILE), 0)
     returns = {}
 
-    def pairs(which, role):
-        if which == 1:
-            know(1, role)
-            beside[role].wait_recv()
-        if (which, role) in direct:
-            direct[which, role].wait_recv()
+    def pairs(which, role, half):
         block_of, rows, info, out = (
             facts[which][role], slots[which][role], notes[which][role], outs[which][role]
         )
         group = pl.ds(4 * role, 4)
-        start_local(rows, sel.at[which, group])
-
-        def body(e, carry):
-            block = vectors[block_of[4 * which + e, 4, 4]]
-            delta = delta_of(mm(block, rows[e], 1, 1), labels, info[4 * which + e])
+        if half == 0:
+            if which == 1 or role == OWN:
+                know(which, role)
+            if (which, role) in direct:
+                direct[which, role].wait_recv()
+            if which == 1 and role != ACROSS:
+                beside[role].wait_recv()
+        if which == 1 and role == ACROSS:
+            beside[role, half].wait_recv()
+        both = (2 * half, 2 * half + 1)
+        blocks = [vectors[block_of[4 * which + e, 4, 4]] for e in both]
+        scores = [mm(block, rows[e], 1, 1) for e, block in zip(both, blocks)]
+        for e, block, score in zip(both, blocks, scores):
+            delta = delta_of(score, labels, info[4 * which + e])
             held_delta[which, 4 * role + e] = delta
             out[e] = mm(delta, block, 0, 0).astype(BF16)
-            return carry
-
-        lax.fori_loop(0, 4, body, 0)
-        start_local(held_delta.at[which, group], deltas.at[which, group])
-        for e in range(3):
-            value = out[e]
-            for f in range(e + 1, 4):
-                same = block_of[4 * which + f, 4, 1] == e
-                value += jnp.where(same, out[f], jnp.zeros((TILE, D), BF16))
-            out[e] = value
-        for e in range(4):
             at = 16 * which + 4 * role + e
             plan[at : at + 1, :] = info[4 * which + e, 4:5, :]
+        if half == 1:
+            start_local(rows, sel.at[which, group])
+            start_local(held_delta.at[which, group], deltas.at[which, group])
+            for e in (2, 1, 0):
+                out[e] = out[e] + out[block_of[4 * which + e, 4, 1]]
 
     row_halves = (pl.ds(0, TILE // 2), pl.ds(TILE // 2, TILE // 2))
     ret_a0, ret_a1, ret_b0, ret_b1 = (a0_0, a0_1), (a1_0, a1_1), (b0_0, b0_1), (b1_0, b1_1)
@@ -363,7 +372,7 @@
             out.at[four, row_halves[r]], back[0][r].at[four], back[1]
         )
 
-    for ref in (out_own, out_x, ret_own, ret_x):
+    for ref in outs[0] + outs[1] + (ret_own, ret_x):
         ref[4] = jnp.zeros((TILE, D), BF16)
     for ref in ret_a0 + ret_a1 + ret_b0 + ret_b1:
         ref[4] = jnp.zeros((TILE // 2, D), BF16)
@@ -435,53 +444,75 @@
             seconda[h, stream].wait_recv()
             ub[h, stream] = rb[h, stream, OWN] + ub[h, stream] + ua[h, stream]
 
+    fetch(0, OWN)
     send_second(BACK)
     send_second(FRONT)
     send_last(BACK, OWN)
     send_second(ACROSS)
-    know(0, OWN)
     for load in load_v:
         wait_local(load)
-    pairs(0, OWN)
+    pairs(0, OWN, 0)
     second_stage(BACK)
     cz_a.wait_recv()
     pos_b = cpall.at[me.x, lax.rem(me.z + b, NZ)]
     cz_f = net.send(pos_b, pos_b, za)
     send_last(FRONT, OWN)
+    pairs(0, OWN, 1)
     second_stage(FRONT)
     across_stage(BACK)
-    pairs(1, OWN)
-    term_in[OWN] = net.send(out1o, ret_own.at[four], sib)
-    across_stage(FRONT)
+    fetch(1, OWN)
+    fetch(0, BACK)
+    fetch(0, FRONT)
     cz_b.wait_recv()
     cz_f.wait_recv()
     pos_row = cpall.at[me.x]
     cx_a = net.send(pos_row, pos_row, xa)
     cx_b = net.send(pos_row, pos_row, xb)
     forward_last(BACK)
+    pairs(1, OWN, 0)
+    across_stage(FRONT)
     send_last(ACROSS, OWN)
     second_stage(ACROSS)
+    pairs(1, OWN, 1)
+    term_in[OWN] = net.send(out1o.at[four], ret_own.at[four], sib)
     complete(BACK)
     pack(BACK)
     across_stage(ACROSS)
+    forward_last(FRONT)
     cx_a.wait_recv()
     pos_row_b = cpall.at[lax.rem(me.x + b, NX)]
     cx_f = net.send(pos_row_b, pos_row_b, xa)
-    pairs(0, BACK)
+    pairs(0, BACK, 0)
+    pairs(0, BACK, 1)
     give_back(0, BACK, 0)
-    forward_last(FRONT)
+    fetch(1, BACK)
+    fetch(1, FRONT)
+    fetch(0, ACROSS)
+    note_in[1, ACROSS] = net.send(no03, no13, sib)
     complete(FRONT)
     pack(FRONT)
-    pairs(0, FRONT)
+    pairs(0, FRONT, 0)
+    pairs(0, FRONT, 1)
     give_back(0, FRONT, 0)
     forward_last(ACROSS)
-    pairs(1, BACK)
+    pairs(1, BACK, 0)
+    pairs(1, BACK, 1)
     give_back(1, BACK, 0)
-    pairs(1, FRONT)
+    fetch(1, ACROSS)
+    pairs(1, FRONT, 0)
+    pairs(1, FRONT, 1)
     give_back(1, FRONT, 0)
     for role in (BACK, FRONT):
         for which in range(2):
             give_back(which, role, 1)
+    complete(ACROSS)
+    pack(ACROSS)
+    pairs(0, ACROSS, 0)
+    pairs(1, ACROSS, 0)
+    pairs(1, ACROSS, 1)
+    term_in[ACROSS] = net.send(out1x.at[four], ret_x.at[four], sib)
+    pairs(0, ACROSS, 1)
+    begin_sum(2)
     wait_local(load_c)
     for j in range(8):
         color, role = j // 4, j % 4
@@ -508,8 +539,19 @@
 
     def rows_coarse(lo, hi):
         def body(t, carry):
-            qt = q_own[t]
-            delta = delta_of(mm(cvm[...], qt, 1, 1), coarse_ids, cpall[t // NZ, lax.rem(t, NZ)])
+            qt = q_own[pl.ds(2 * t, 2)].reshape(2 * TILE, D)
+            scores = mm(cvm[...], qt, 1, 1)
+            delta = jnp.concatenate(
+                [
+                    delta_of(
+                        scores[:, h * TILE : (h + 1) * TILE],
+                        coarse_ids,
+                        cpall[t // 2, 2 * lax.rem(t, 2) + h],
+                    )
+                    for h in range(2)
+                ],
+                axis=1,
+            )
             gc[...] += mm(delta, qt, 1, 0)
             return carry
 
@@ -517,25 +559,19 @@
 
 
     gc[...] = jnp.zeros_like(gc)
-    own_coarse()
-    complete(ACROSS)
-    pack(ACROSS)
     cx_b.wait_recv()
     cx_f.wait_recv()
-    pairs(0, ACROSS)
-    rows_coarse(0, 8)
-    pairs(1, ACROSS)
-    term_in[ACROSS] = net.send(out1x, ret_x.at[four], sib)
-    rows_coarse(8, 16)
-    coarse = net.send(gc.at[pl.ds(64 * (1 - c), 64)], gsib, sib)
-    begin_sum(2)
+    rows_coarse(0, 4)
     begin_sum(0)
     begin_sum(1)
     pass_sum(2)
+    rows_coarse(4, 8)
+    coarse = net.send(gc.at[pl.ds(64 * (1 - c), 64)], gsib, sib)
     pass_sum(0)
     pass_sum(1)
     begin_sum(3)
     begin_second(2)
+    own_coarse()
     begin_second(0)
     begin_second(1)
     pass_sum(3)
@@ -721,7 +757,7 @@
             pltpu.VMEM((40, 128), jnp.int32),
             pltpu.SMEM((40, 128), jnp.int32),
             near, near, near, near, four, four, rest, rest,
-            five, five, four, four, four, four, four, four,
+            five, five, five, five, five, five, five, five,
             five, five,
             half, half, half, half, half, half, half, half,
             pltpu.VMEM((6, BLOCK, D), BF16),

time: 135 us -> 119 us (0.88)
  Pallas kernels: 132 us -> 117 us
    pallas_call x1, Pallas kernels: 123 us -> 108 us  [shards(): pl.pallas_call(main_kernel, out_shape=(shape((TILE, D), F32), shape((16,...]
where the time goes in v4:
time: 119 us
  Pallas kernels  117 us (98%)
  local copies, waits for them, and re-layouts  1.38 us (1%)
    pallas_call x1, Pallas kernels, shards(): pl.pallas_call(main_kernel, out_shape=(shape((TILE, D), F32), shape((16,...  108 us
    pallas_call x1, Pallas kernels, shards(): pl.pallas_call(grads_kernel, out_shape=(shape((4, BLOCK, D), F32), shape(...  9.27 us

profile of v4, /device:TPU:0, one launch (start us, length us, event | category | flops | bytes accessed | tf_op | source)
XLA Modules:
  0.0 119.0 jit_solution(6188700589206764553)
XLA Ops:
  0.6 107.7 %main.1 = (f32[128,768]{1,0:T(8,128)}, f32[16,768]{1,0:T(8,128)}, s32[32,128]{1,0:T(8,128)}, bf16[2,16,128,768]{3,2,1,0:T(8,128)(2,1)}, bf16[2,16,512,128]{3,2,1,0:T(8,128)(2,1)}) custom-call(bf16[16,128,768]{2,1,0:T(8,128)(2,1)} %bitcast.15, s32[4,2048]{1,0:T(4,128)} %bitcast.18, s32[4,2048]{1,0:T(4,128)} %bitcast.19, s32[8,16]{1,0:T(8,128)} %bitcast.20, ...), custom_call_target="tpu_custom_call" | custom-call | tf_op jit(solution)/shard_map/main/pallas_call | solution.py:736
  108.3 0.0 copy-start
  108.4 0.0 copy-start.1
  108.4 9.3 %grads.1 = (f32[4,512,768]{2,1,0:T(8,128)}, f32[2,512,768]{2,1,0:T(8,128)}) custom-call(s32[32,128]{1,0:T(8,128)} %get-tuple-element.13.plan, bf16[32,128,768]{2,1,0:T(8,128)(2,1)} %bitcast.13, bf16[32,512,128]{2,1,0:T(8,128)(2,1)} %bitcast.14), custom_call_target="tpu_custom_call" | custom-call | tf_op jit(solution)/shard_map/grads/pallas_call | solution.py:792
  117.6 0.0 copy-done
  117.6 0.7 copy.16
  118.4 0.0 copy-done.1
  118.4 0.6 copy.17
Async XLA Ops:
  108.3 9.3 %copy-start = (f32[128,768]{1,0:T(8,128)S(1)}, f32[128,768]{1,0:T(8,128)}, u32[]{:S(2)}) copy-start(f32[128,768]{1,0:T(8,128)} %get-tuple-element.22) | copy-start | bytes 1179652
  108.4 10.0 %copy-start.1 = (f32[16,768]{1,0:T(8,128)S(1)}, f32[16,768]{1,0:T(8,128)}, u32[]{:S(2)}) copy-start(f32[16,768]{1,0:T(8,128)} %get-tuple-element.23) | copy-start | bytes 147460

commit v5 on v4

--- a/solution.py
+++ b/solution.py
@@ -18,7 +18,7 @@
 MESH = pl.DeviceIdType.MESH
 THIRD = D // 3
 HALF = D // 2
-NEAR = 64
+NEAR = 96
 REST = TILE - NEAR
 
 
@@ -105,7 +105,7 @@
     sm00, sm01, sm02, sm03, sm10, sm11, sm12, sm13,
     no_a, no_b, no_x, planv, smo, pk_as, pk_ao, pk_bs, pk_bo, pk_own, pk_x, pk_b, pk_f,
     out_own, out_x, out0b, out0f, out1o, out1b, out1f, out1x,
-    ret_own, ret_x, a0_0, a0_1, a1_0, a1_1, b0_0, b0_1, b1_0, b1_1,
+    ret_own, x_0, x_1, a0_0, a0_1, a1_0, a1_1, b0_0, b0_1, b1_0, b1_1,
     vectors, held_delta, gc, qc, gsib, gbuf,
     s2, sb, r2, rb, ra, u2, ub, ua, far, local_sem, send_sem, recv_sem,
 ):
@@ -358,6 +358,7 @@
 
     row_halves = (pl.ds(0, TILE // 2), pl.ds(TILE // 2, TILE // 2))
     ret_a0, ret_a1, ret_b0, ret_b1 = (a0_0, a0_1), (a1_0, a1_1), (b0_0, b0_1), (b1_0, b1_1)
+    ret_x = (x_0, x_1)
     four = pl.ds(0, 4)
 
     def give_back(which, role, r):
@@ -372,9 +373,9 @@
             out.at[four, row_halves[r]], back[0][r].at[four], back[1]
         )
 
-    for ref in outs[0] + outs[1] + (ret_own, ret_x):
+    for ref in outs[0] + outs[1] + (ret_own,):
         ref[4] = jnp.zeros((TILE, D), BF16)
-    for ref in ret_a0 + ret_a1 + ret_b0 + ret_b1:
+    for ref in ret_x + ret_a0 + ret_a1 + ret_b0 + ret_b1:
         ref[4] = jnp.zeros((TILE // 2, D), BF16)
     steps = (0, b, a, 2)
     first_axis = ((xa, xb), (za, zb))
@@ -388,7 +389,7 @@
         r = stream % 2
         rows = slice(r * TILE // 2, (r + 1) * TILE // 2)
         if stream < 2:
-            return out_x[sm03[8, 0, tile], rows, cols] + ret_x[sm03[8, 1, tile], rows, cols]
+            return out_x[sm03[8, 0, tile], rows, cols] + ret_x[r][sm03[8, 1, tile], :, cols]
         value = out_own[smo[32 + 2 * OWN, tile], rows, cols]
         value += ret_own[smo[33 + 2 * OWN, tile], rows, cols]
         value += ret_a0[r][smo[32 + 2 * BACK, tile], :, cols]
@@ -397,8 +398,8 @@
         return value + ret_b1[r][smo[33 + 2 * FRONT, tile], :, cols]
 
     def begin_sum(stream):
-        if stream == 0:
-            term_in[ACROSS].wait_recv()
+        if stream < 2:
+            term_in[ACROSS, stream].wait_recv()
         if stream >= 2:
             if stream == 2:
                 term_in[OWN].wait_recv()
@@ -510,7 +511,8 @@
     pairs(0, ACROSS, 0)
     pairs(1, ACROSS, 0)
     pairs(1, ACROSS, 1)
-    term_in[ACROSS] = net.send(out1x.at[four], ret_x.at[four], sib)
+    for r in range(2):
+        term_in[ACROSS, r] = net.send(out1x.at[four, row_halves[r]], ret_x[r].at[four], sib)
     pairs(0, ACROSS, 1)
     begin_sum(2)
     wait_local(load_c)
@@ -611,10 +613,16 @@
 
 
 def grads_kernel(
-    plan, sel, deltas,
-    gm, gl,
-    counts, entries, rows, held, acc, row_sem, delta_sem, grad_sem,
+    plan, sel, deltas, gq_in, gco_in,
+    gm, gl, gq, gco,
+    counts, entries, rows, held, acc, row_sem, delta_sem, grad_sem, out_sem,
 ):
+    results = [
+        pltpu.make_async_copy(gq_in, gq, out_sem.at[0]),
+        pltpu.make_async_copy(gco_in, gco, out_sem.at[1]),
+    ]
+    for copy in results:
+        copy.start()
     stores = [(gm, 0), (gm, 1), (gm, 2), (gm, 3), (gl, 0), (gl, 1)]
 
     def row_copy(e):
@@ -690,6 +698,8 @@
     lax.fori_loop(0, 6, per_key, 0)
     for i, (out, j) in enumerate(stores):
         pltpu.make_async_copy(acc.at[i], out.at[j], grad_sem.at[i]).wait()
+    for copy in results:
+        copy.wait()
 
 
 def vmem():
@@ -758,8 +768,8 @@
             pltpu.SMEM((40, 128), jnp.int32),
             near, near, near, near, four, four, rest, rest,
             five, five, five, five, five, five, five, five,
-            five, five,
-            half, half, half, half, half, half, half, half,
+            five,
+            half, half, half, half, half, half, half, half, half, half,
             pltpu.VMEM((6, BLOCK, D), BF16),
             pltpu.VMEM((2, 16, BLOCK, TILE), BF16),
             pltpu.VMEM((128, D), F32),
@@ -789,11 +799,16 @@
         mid_vectors.reshape(4, BLOCK, D),
         leaf_vectors.reshape(2, BLOCK, D),
     )
-    gm, gl = pl.pallas_call(
+    gm, gl, gq, gco = pl.pallas_call(
         grads_kernel,
-        out_shape=(shape((4, BLOCK, D), F32), shape((2, BLOCK, D), F32)),
-        in_specs=[smem(), hbm(), hbm()],
-        out_specs=(hbm(), hbm()),
+        out_shape=(
+            shape((4, BLOCK, D), F32),
+            shape((2, BLOCK, D), F32),
+            shape((TILE, D), F32),
+            shape((16, D), F32),
+        ),
+        in_specs=[smem(), hbm(), hbm(), hbm(), hbm()],
+        out_specs=(hbm(), hbm(), hbm(), hbm()),
         scratch_shapes=[
             pltpu.SMEM((6,), jnp.int32),
             pltpu.SMEM((6 * LIST + 1,), jnp.int32),
@@ -803,10 +818,11 @@
             dma((SLOTS,)),
             dma((SLOTS,)),
             dma((6,)),
+            dma((2,)),
         ],
         compiler_params=pltpu.CompilerParams(vmem_limit_bytes=60 * mib),
         name="grads",
-    )(plan, sel.reshape(SLOTS, TILE, D), deltas.reshape(SLOTS, BLOCK, TILE))
+    )(plan, sel.reshape(SLOTS, TILE, D), deltas.reshape(SLOTS, BLOCK, TILE), gq, gco)
     return gq, gco, gm.reshape(4 * BLOCK, D), gl.reshape(2 * BLOCK, D)
 
 

time: 119 us -> 123 us (1.034)
  Pallas kernels: 117 us -> 122 us
  local copies, waits for them, and re-layouts: 1.38 us -> 0 us
    pallas_call x1, Pallas kernels: 9.27 us -> 16.1 us  [shards(): pl.pallas_call(grads_kernel, out_shape=(shape((4, BLOCK, D), F32), shape(...]
    pallas_call x1, Pallas kernels: 108 us -> 106 us  [shards(): pl.pallas_call(main_kernel, out_shape=(shape((TILE, D), F32), shape((16,...]
    unnamed x6 -> x0, local copies, waits for them, and re-layouts: 1.38 us -> none
where the time goes in v5:
time: 123 us
  Pallas kernels  122 us (99%)
    pallas_call x1, Pallas kernels, shards(): pl.pallas_call(main_kernel, out_shape=(shape((TILE, D), F32), shape((16,...  106 us
    pallas_call x1, Pallas kernels, shards(): pl.pallas_call(grads_kernel, out_shape=(shape((4, BLOCK, D), F32), shape(...  16.1 us

profile of v5, /device:TPU:0, one launch (start us, length us, event | category | flops | bytes accessed | tf_op | source)
XLA Modules:
  0.0 122.6 jit_solution(5132218268378497117)
XLA Ops:
  0.6 105.7 %main.1 = (f32[128,768]{1,0:T(8,128)}, f32[16,768]{1,0:T(8,128)}, s32[32,128]{1,0:T(8,128)}, bf16[2,16,128,768]{3,2,1,0:T(8,128)(2,1)}, bf16[2,16,512,128]{3,2,1,0:T(8,128)(2,1)}) custom-call(bf16[16,128,768]{2,1,0:T(8,128)(2,1)} %bitcast.15, s32[4,2048]{1,0:T(4,128)} %bitcast.18, s32[4,2048]{1,0:T(4,128)} %bitcast.19, s32[8,16]{1,0:T(8,128)} %bitcast.20, ...), custom_call_target="tpu_custom_call" | custom-call | tf_op jit(solution)/shard_map/main/pallas_call | solution.py:746
  106.4 16.1 %grads.1 = (f32[4,512,768]{2,1,0:T(8,128)}, f32[2,512,768]{2,1,0:T(8,128)}, f32[128,768]{1,0:T(8,128)}, f32[16,768]{1,0:T(8,128)}) custom-call(s32[32,128]{1,0:T(8,128)} %get-tuple-element.13.plan, bf16[32,128,768]{2,1,0:T(8,128)(2,1)} %bitcast.13, bf16[32,512,128]{2,1,0:T(8,128)(2,1)} %bitcast.14, f32[128,768]{1,0:T(8,128)} %get-tuple-element.16.gq_in, ...), custom_call_target="tpu_custom_call" | custom-call | tf_op jit(solution)/shard_map/grads/pallas_call | solution.py:802

commit v6 on v5

--- a/solution.py
+++ b/solution.py
@@ -65,7 +65,7 @@
 
 class Net:
     def __init__(self, send_sem, recv_sem):
-        self.send_sem, self.recv_sem, self.made = send_sem, recv_sem, []
+        self.send_sem, self.recv_sem, self.made, self.drained = send_sem, recv_sem, [], 0
 
     def send(self, src, dst, device):
         i = len(self.made)
@@ -81,9 +81,10 @@
         self.made.append(copy)
         return copy
 
-    def finish(self):
-        for copy in self.made:
+    def drain(self, count):
+        for copy in self.made[self.drained : count]:
             copy.wait_send()
+        self.drained = count
 
 
 COPIES = 200
@@ -171,7 +172,8 @@
     def whole(value):
         return jnp.broadcast_to(value, (1, 128))
 
-    for label, step in enumerate((0, a, b, 2)):
+    def plan_slots(label):
+        step = (0, a, b, 2)[label]
         for which, core in enumerate((c, 1 - c)):
             device = (2 * lax.rem(me.y + step, NY) + core) * TILES + m
             held = [
@@ -210,6 +212,9 @@
                 row = jnp.where(lane == 4, (value & 3) + 4 * (e // 2), row)
                 at = 8 * label + 4 * which + e
                 planv[at : at + 1, :] = row
+    planv[...] = jnp.zeros((40, 128), jnp.int32)
+    plan_slots(BACK)
+    plan_slots(FRONT)
     to_smem = start_local(planv, smo)
     wait_local(load_q)
     wait_local(to_smem)
@@ -235,6 +240,10 @@
                 buffer[e] = q_own[smo[8 * label + 4 * which + e, 2], 0:NEAR]
             note_in[which, label] = net.send(notes_out[label], notes[which][label], device)
             direct[which, label] = net.send(buffer, slots[which][label].at[:, near], device)
+    plan_slots(ACROSS)
+    plan_slots(OWN)
+    to_smem = start_local(planv, smo)
+    wait_local(to_smem)
     fill_notes(ACROSS)
     note_in[0, ACROSS] = net.send(no_x, no03, across)
     fill_notes(OWN)
@@ -493,9 +502,11 @@
     complete(FRONT)
     pack(FRONT)
     pairs(0, FRONT, 0)
+    forward_last(ACROSS)
     pairs(0, FRONT, 1)
     give_back(0, FRONT, 0)
-    forward_last(ACROSS)
+    complete(ACROSS)
+    pack(ACROSS)
     pairs(1, BACK, 0)
     pairs(1, BACK, 1)
     give_back(1, BACK, 0)
@@ -506,15 +517,14 @@
     for role in (BACK, FRONT):
         for which in range(2):
             give_back(which, role, 1)
-    complete(ACROSS)
-    pack(ACROSS)
-    pairs(0, ACROSS, 0)
     pairs(1, ACROSS, 0)
     pairs(1, ACROSS, 1)
     for r in range(2):
         term_in[ACROSS, r] = net.send(out1x.at[four, row_halves[r]], ret_x[r].at[four], sib)
+    pairs(0, ACROSS, 0)
     pairs(0, ACROSS, 1)
     begin_sum(2)
+    early = len(net.made)
     wait_local(load_c)
     for j in range(8):
         color, role = j // 4, j % 4
@@ -577,6 +587,10 @@
     begin_second(0)
     begin_second(1)
     pass_sum(3)
+    net.drain(early)
+    for copy in local:
+        if not any(copy is other for other in done):
+            wait_local(copy)
     pass_second(2)
     pass_second(0)
     pass_second(1)
@@ -609,7 +623,7 @@
     for copy in local:
         if not any(copy is other for other in done):
             copy.wait()
-    net.finish()
+    net.drain(len(net.made))
 
 
 def grads_kernel(
@@ -807,7 +821,7 @@
             shape((TILE, D), F32),
             shape((16, D), F32),
         ),
-        in_specs=[smem(), hbm(), hbm(), hbm(), hbm()],
+        in_specs=[smem(), hbm(), hbm(), vmem(), vmem()],
         out_specs=(hbm(), hbm(), hbm(), hbm()),
         scratch_shapes=[
             pltpu.SMEM((6,), jnp.int32),

time: 123 us -> 123 us (level)
    pallas_call x1, Pallas kernels: 106 us -> 111 us  [shards(): pl.pallas_call(main_kernel, out_shape=(shape((TILE, D), F32), shape((16,...]
    pallas_call x1, Pallas kernels: 16.1 us -> 10.8 us  [shards(): pl.pallas_call(grads_kernel, out_shape=(shape((4, BLOCK, D), F32), shape(...]
where the time goes in v6:
time: 123 us
  Pallas kernels  122 us (99%)
    pallas_call x1, Pallas kernels, shards(): pl.pallas_call(main_kernel, out_shape=(shape((TILE, D), F32), shape((16,...  111 us
    pallas_call x1, Pallas kernels, shards(): pl.pallas_call(grads_kernel, out_shape=(shape((4, BLOCK, D), F32), shape(...  10.8 us

profile of v6, /device:TPU:0, one launch (start us, length us, event | category | flops | bytes accessed | tf_op | source)
XLA Modules:
  0.0 122.7 jit_solution(3074926194219080003)
XLA Ops:
  0.6 111.1 %main.1 = (f32[128,768]{1,0:T(8,128)}, f32[16,768]{1,0:T(8,128)}, s32[32,128]{1,0:T(8,128)}, bf16[2,16,128,768]{3,2,1,0:T(8,128)(2,1)}, bf16[2,16,512,128]{3,2,1,0:T(8,128)(2,1)}) custom-call(bf16[16,128,768]{2,1,0:T(8,128)(2,1)} %bitcast.15, s32[4,2048]{1,0:T(4,128)} %bitcast.18, s32[4,2048]{1,0:T(4,128)} %bitcast.19, s32[8,16]{1,0:T(8,128)} %bitcast.20, ...), custom_call_target="tpu_custom_call" | custom-call | tf_op jit(solution)/shard_map/main/pallas_call | solution.py:760
  111.8 10.8 %grads.1 = (f32[4,512,768]{2,1,0:T(8,128)}, f32[2,512,768]{2,1,0:T(8,128)}, f32[128,768]{1,0:T(8,128)}, f32[16,768]{1,0:T(8,128)}) custom-call(s32[32,128]{1,0:T(8,128)} %get-tuple-element.13.plan, bf16[32,128,768]{2,1,0:T(8,128)(2,1)} %bitcast.13, bf16[32,512,128]{2,1,0:T(8,128)(2,1)} %bitcast.14, f32[128,768]{1,0:T(8,128)} %get-tuple-element.16.gq_in, ...), custom_call_target="tpu_custom_call" | custom-call | tf_op jit(solution)/shard_map/grads/pallas_call | solution.py:816

commit v7 on v6

--- a/solution.py
+++ b/solution.py
@@ -502,11 +502,9 @@
     complete(FRONT)
     pack(FRONT)
     pairs(0, FRONT, 0)
-    forward_last(ACROSS)
     pairs(0, FRONT, 1)
     give_back(0, FRONT, 0)
-    complete(ACROSS)
-    pack(ACROSS)
+    forward_last(ACROSS)
     pairs(1, BACK, 0)
     pairs(1, BACK, 1)
     give_back(1, BACK, 0)
@@ -517,11 +515,13 @@
     for role in (BACK, FRONT):
         for which in range(2):
             give_back(which, role, 1)
+    complete(ACROSS)
+    pack(ACROSS)
+    pairs(0, ACROSS, 0)
     pairs(1, ACROSS, 0)
     pairs(1, ACROSS, 1)
     for r in range(2):
         term_in[ACROSS, r] = net.send(out1x.at[four, row_halves[r]], ret_x[r].at[four], sib)
-    pairs(0, ACROSS, 0)
     pairs(0, ACROSS, 1)
     begin_sum(2)
     early = len(net.made)
@@ -587,10 +587,6 @@
     begin_second(0)
     begin_second(1)
     pass_sum(3)
-    net.drain(early)
-    for copy in local:
-        if not any(copy is other for other in done):
-            wait_local(copy)
     pass_second(2)
     pass_second(0)
     pass_second(1)
@@ -608,6 +604,10 @@
     gbuf[4] = gbuf[FRONT] + gbuf[5]
     coarsea = net.send(gbuf.at[4], gbuf.at[7], up)
     pass_second(3)
+    net.drain(early)
+    for copy in local:
+        if not any(copy is other for other in done):
+            wait_local(copy)
     coarsea.wait_recv()
     coarseb.wait_recv()
     gco[...] = gbuf[OWN] + gbuf[6] + gbuf[7]

time: 123 us -> 117 us (0.951); the launches traced: 123 us -> 115 us
  Pallas kernels: 122 us -> 114 us
    pallas_call x1, Pallas kernels: 111 us -> 106 us  [shards(): pl.pallas_call(main_kernel, out_shape=(shape((TILE, D), F32), shape((16,...]
    pallas_call x1, Pallas kernels: 10.8 us -> 8.69 us  [shards(): pl.pallas_call(grads_kernel, out_shape=(shape((4, BLOCK, D), F32), shape(...]
where the time goes in v7:
time: 117 us; the launch traced here: 115 us
  Pallas kernels  114 us (97%)
    pallas_call x1, Pallas kernels, shards(): pl.pallas_call(main_kernel, out_shape=(shape((TILE, D), F32), shape((16,...  106 us
    pallas_call x1, Pallas kernels, shards(): pl.pallas_call(grads_kernel, out_shape=(shape((4, BLOCK, D), F32), shape(...  8.69 us

profile of v7, /device:TPU:0, one launch (start us, length us, event | category | flops | bytes accessed | tf_op | source)
XLA Modules:
  0.0 115.0 jit_solution(10832604012460868633)
XLA Ops:
  0.6 105.5 %main.1 = (f32[128,768]{1,0:T(8,128)}, f32[16,768]{1,0:T(8,128)}, s32[32,128]{1,0:T(8,128)}, bf16[2,16,128,768]{3,2,1,0:T(8,128)(2,1)}, bf16[2,16,512,128]{3,2,1,0:T(8,128)(2,1)}) custom-call(bf16[16,128,768]{2,1,0:T(8,128)(2,1)} %bitcast.15, s32[4,2048]{1,0:T(4,128)} %bitcast.18, s32[4,2048]{1,0:T(4,128)} %bitcast.19, s32[8,16]{1,0:T(8,128)} %bitcast.20, ...), custom_call_target="tpu_custom_call" | custom-call | tf_op jit(solution)/shard_map/main/pallas_call | solution.py:760
  106.1 8.7 %grads.1 = (f32[4,512,768]{2,1,0:T(8,128)}, f32[2,512,768]{2,1,0:T(8,128)}, f32[128,768]{1,0:T(8,128)}, f32[16,768]{1,0:T(8,128)}) custom-call(s32[32,128]{1,0:T(8,128)} %get-tuple-element.13.plan, bf16[32,128,768]{2,1,0:T(8,128)(2,1)} %bitcast.13, bf16[32,512,128]{2,1,0:T(8,128)(2,1)} %bitcast.14, f32[128,768]{1,0:T(8,128)} %get-tuple-element.16.gq_in, ...), custom_call_target="tpu_custom_call" | custom-call | tf_op jit(solution)/shard_map/grads/pallas_call | solution.py:816

commit v8 on v7

--- a/solution.py
+++ b/solution.py
@@ -18,7 +18,7 @@
 MESH = pl.DeviceIdType.MESH
 THIRD = D // 3
 HALF = D // 2
-NEAR = 96
+NEAR = 64
 REST = TILE - NEAR
 
 
@@ -523,7 +523,6 @@
     for r in range(2):
         term_in[ACROSS, r] = net.send(out1x.at[four, row_halves[r]], ret_x[r].at[four], sib)
     pairs(0, ACROSS, 1)
-    begin_sum(2)
     early = len(net.made)
     wait_local(load_c)
     for j in range(8):
@@ -576,20 +575,21 @@
     rows_coarse(0, 4)
     begin_sum(0)
     begin_sum(1)
-    pass_sum(2)
+    begin_sum(2)
     rows_coarse(4, 8)
     coarse = net.send(gc.at[pl.ds(64 * (1 - c), 64)], gsib, sib)
     pass_sum(0)
     pass_sum(1)
+    pass_sum(2)
+    own_coarse()
     begin_sum(3)
-    begin_second(2)
-    own_coarse()
     begin_second(0)
     begin_second(1)
+    begin_second(2)
     pass_sum(3)
-    pass_second(2)
     pass_second(0)
     pass_second(1)
+    pass_second(2)
     coarse.wait_recv()
     for role in range(4):
         gbuf[role] = gc[pl.ds(64 * c + 16 * role, 16)] + gsib[16 * role : 16 * role + 16]

time: 117 us -> 116 us (level); the launches traced: 115 us -> 115 us
  no operation moved by 1% of the time
where the time goes in v8:
time: 116 us; the launch traced here: 115 us
  Pallas kernels  114 us (98%)
    pallas_call x1, Pallas kernels, shards(): pl.pallas_call(main_kernel, out_shape=(shape((TILE, D), F32), shape((16,...  106 us
    pallas_call x1, Pallas kernels, shards(): pl.pallas_call(grads_kernel, out_shape=(shape((4, BLOCK, D), F32), shape(...  8.38 us

profile of v8, /device:TPU:0, one launch (start us, length us, event | category | flops | bytes accessed | tf_op | source)
XLA Modules:
  0.0 115.2 jit_solution(14635203031515220105)
XLA Ops:
  0.6 106.0 %main.1 = (f32[128,768]{1,0:T(8,128)}, f32[16,768]{1,0:T(8,128)}, s32[32,128]{1,0:T(8,128)}, bf16[2,16,128,768]{3,2,1,0:T(8,128)(2,1)}, bf16[2,16,512,128]{3,2,1,0:T(8,128)(2,1)}) custom-call(bf16[16,128,768]{2,1,0:T(8,128)(2,1)} %bitcast.15, s32[4,2048]{1,0:T(4,128)} %bitcast.18, s32[4,2048]{1,0:T(4,128)} %bitcast.19, s32[8,16]{1,0:T(8,128)} %bitcast.20, ...), custom_call_target="tpu_custom_call" | custom-call | tf_op jit(solution)/shard_map/main/pallas_call | solution.py:760
  106.6 8.4 %grads.1 = (f32[4,512,768]{2,1,0:T(8,128)}, f32[2,512,768]{2,1,0:T(8,128)}, f32[128,768]{1,0:T(8,128)}, f32[16,768]{1,0:T(8,128)}) custom-call(s32[32,128]{1,0:T(8,128)} %get-tuple-element.13.plan, bf16[32,128,768]{2,1,0:T(8,128)(2,1)} %bitcast.13, bf16[32,512,128]{2,1,0:T(8,128)(2,1)} %bitcast.14, f32[128,768]{1,0:T(8,128)} %get-tuple-element.16.gq_in, ...), custom_call_target="tpu_custom_call" | custom-call | tf_op jit(solution)/shard_map/grads/pallas_call | solution.py:816

commit v9 on v8

--- a/solution.py
+++ b/solution.py
@@ -504,6 +504,8 @@
     pairs(0, FRONT, 0)
     pairs(0, FRONT, 1)
     give_back(0, FRONT, 0)
+    give_back(0, BACK, 1)
+    give_back(0, FRONT, 1)
     forward_last(ACROSS)
     pairs(1, BACK, 0)
     pairs(1, BACK, 1)
@@ -512,9 +514,8 @@
     pairs(1, FRONT, 0)
     pairs(1, FRONT, 1)
     give_back(1, FRONT, 0)
-    for role in (BACK, FRONT):
-        for which in range(2):
-            give_back(which, role, 1)
+    give_back(1, BACK, 1)
+    give_back(1, FRONT, 1)
     complete(ACROSS)
     pack(ACROSS)
     pairs(0, ACROSS, 0)

time: 116 us -> 120 us (1.034)
  the two profiles are of different devices: /device:TPU:0 before, /device:TPU:8 now
where the time goes in v9:
time: 120 us; the launch traced here: 119 us
  Pallas kernels  118 us (98%)
    pallas_call x1, Pallas kernels, shards(): pl.pallas_call(main_kernel, out_shape=(shape((TILE, D), F32), shape((16,...  109 us
    pallas_call x1, Pallas kernels, shards(): pl.pallas_call(grads_kernel, out_shape=(shape((4, BLOCK, D), F32), shape(...  8.56 us

profile of v9, /device:TPU:8, one launch (start us, length us, event | category | flops | bytes accessed | tf_op | source)
XLA Modules:
  0.0 118.7 jit_solution(13299169090954995365)
XLA Ops:
  0.6 109.3 %main.1 = (f32[128,768]{1,0:T(8,128)}, f32[16,768]{1,0:T(8,128)}, s32[32,128]{1,0:T(8,128)}, bf16[2,16,128,768]{3,2,1,0:T(8,128)(2,1)}, bf16[2,16,512,128]{3,2,1,0:T(8,128)(2,1)}) custom-call(bf16[16,128,768]{2,1,0:T(8,128)(2,1)} %bitcast.15, s32[4,2048]{1,0:T(4,128)} %bitcast.18, s32[4,2048]{1,0:T(4,128)} %bitcast.19, s32[8,16]{1,0:T(8,128)} %bitcast.20, ...), custom_call_target="tpu_custom_call" | custom-call | tf_op jit(solution)/shard_map/main/pallas_call | solution.py:761
  109.9 8.6 %grads.1 = (f32[4,512,768]{2,1,0:T(8,128)}, f32[2,512,768]{2,1,0:T(8,128)}, f32[128,768]{1,0:T(8,128)}, f32[16,768]{1,0:T(8,128)}) custom-call(s32[32,128]{1,0:T(8,128)} %get-tuple-element.13.plan, bf16[32,128,768]{2,1,0:T(8,128)(2,1)} %bitcast.13, bf16[32,512,128]{2,1,0:T(8,128)(2,1)} %bitcast.14, f32[128,768]{1,0:T(8,128)} %get-tuple-element.16.gq_in, ...), custom_call_target="tpu_custom_call" | custom-call | tf_op jit(solution)/shard_map/grads/pallas_call | solution.py:817
